TPU v7x, 32 devices: a whole 2x2x4 slice. The times are simulated.
32 devices in a mesh: row: 4 (over x, core), col: 8 (over z, y).
Axes of the slice: x: 2, y: 2, z: 4, core: 2. Of those that a mesh axis runs over, the one named last changes fastest.
Arguments:
- scalar_field: bfloat16 [768, 768, 1024], P('row', 'col'), may hold values from -6 to 6
- x_operator: bfloat16 [1024, 1024], replicated, may hold values from -0.1875 to 0.1875
- y_second: bfloat16 [768, 768], replicated, may hold values from -0.21875 to 0.21875
- y_first: bfloat16 [768, 768], replicated, may hold values from -0.21875 to 0.21875
- y_stretch: float32 [768], replicated, may hold values from 0.5 to 2
- y_curve: float32 [768], replicated, may hold values from -3 to 3
- z_operator: bfloat16 [768, 768], replicated, may hold values from -0.21875 to 0.21875
Outputs:
- diffusion: bfloat16 [768, 768, 1024], P('row', 'col')
All inputs are finite; a program needn't handle non-finite values.
Results may differ from a plain program's by a relative error of at most 0.0052.
Values may be sent and summed in bfloat16 or wider, within the bound.
No kernel may reach another device: no remote copies, remote signals or barrier semaphores. Data moves between devices by JAX's collectives and lax.ppermute only.
A program may use at most 384 MiB of HBM per device.

v0:
```python
import jax
import jax.numpy as jnp
from jax import lax
from jax.sharding import PartitionSpec as P


def x_apply(scalar_field, x_operator):
    flat = scalar_field.reshape(-1, scalar_field.shape[2])
    product = jnp.dot(flat, x_operator, preferred_element_type=jnp.float32)
    return product.reshape(scalar_field.shape[0], scalar_field.shape[1], x_operator.shape[1])


def per_device(scalar_field, x_operator, y_second, y_first, y_stretch, y_curve, z_operator):
    y_combined = (
        y_stretch[None, :] * y_second.astype(jnp.float32)
        + y_curve[None, :] * y_first.astype(jnp.float32)
    ).astype(jnp.bfloat16)
    x_term = x_apply(scalar_field, x_operator)
    columns = lax.all_to_all(scalar_field, "row", split_axis=2, concat_axis=0, tiled=True)
    y_term = jnp.einsum("yzx,yk->kzx", columns, y_combined, preferred_element_type=jnp.float32)
    pencil_y, y_term = (columns, y_term.astype(jnp.bfloat16))
    pencil_z = lax.all_to_all(pencil_y, "col", split_axis=0, concat_axis=1, tiled=True)
    z_full = jnp.einsum("yzx,zk->ykx", pencil_z, z_operator, preferred_element_type=jnp.float32)
    z_in_y = lax.all_to_all(
        z_full.astype(jnp.bfloat16), "col", split_axis=1, concat_axis=0, tiled=True
    )
    y_back, z_back = (
        lax.all_to_all(y_term, "row", split_axis=0, concat_axis=2, tiled=True),
        lax.all_to_all(z_in_y, "row", split_axis=0, concat_axis=2, tiled=True),
    )
    total = x_term + y_back.astype(jnp.float32) + z_back.astype(jnp.float32)
    return total.astype(jnp.bfloat16)


def solution(mesh):
    in_specs = (P("row", "col", None), P(), P(), P(), P(), P(), P())
    out_specs = P("row", "col", None)
    return jax.shard_map(
        per_device, mesh=mesh, in_specs=in_specs, out_specs=out_specs, check_vma=False
    )
```

profile of v0, /device:TPU:0, one launch (start us, length us, event | category | flops | bytes accessed | tf_op | source)
XLA Modules:
  0.0 3472.0 jit_solution(5528770836698614285)
XLA Ops:
  0.0 0.0 copy-start
  0.0 58.1 %copy.30 = bf16[192,96,1024]{1,0,2:T(8,128)(2,1)} copy(bf16[192,96,1024]{2,1,0:T(8,128)(2,1)} %param.7) | data formatting | bytes 75497472 | tf_op args[0]
  58.1 568.4 %all_to_all.72 = bf16[192,96,1024]{1,0,2:T(8,128)(2,1)} all-to-all(bf16[192,96,1024]{1,0,2:T(8,128)(2,1)} %copy.30), channel_id=1, replica_groups=mesh['row'=4,'col'=8] {'row'}, dimensions={2} | all-to-all | bytes 75497472 | tf_op jit(solution)/shard_map/all_to_all | solution.py:19
  626.5 65.9 %copy.31 = bf16[192,96,4,256]{3,0,2,1:T(8,128)(2,1)} copy(bf16[192,96,4,256]{1,0,3,2:T(8,128)(2,1)} %bitcast.40) | data formatting | bytes 75497472 | tf_op jit(solution)/shard_map/all_to_all | solution.py:19
  692.4 34.9 %copy.35 = bf16[768,96,256]{2,1,0:T(8,128)(2,1)} copy(bf16[768,96,256]{2,0,1:T(8,128)(2,1)} %bitcast.43) | data formatting | bytes 75497472 | tf_op jit(solution)/shard_map/all_to_all | solution.py:19
  727.3 824.9 %all_to_all.73 = bf16[768,96,256]{2,1,0:T(8,128)(2,1)} all-to-all(bf16[768,96,256]{2,1,0:T(8,128)(2,1)} %copy.35), channel_id=1, replica_groups=mesh['row'=4,'col'=8] {'col'}, dimensions={0} | all-to-all | bytes 75497472 | tf_op jit(solution)/shard_map/all_to_all | solution.py:22
  1552.2 0.0 copy-start.1
  1552.2 25.6 copy.36
  1577.8 0.0 copy-done.1
  1577.9 44.9 %convert_bitcast_fusion.1 = bf16[96,768,256]{2,1,0:T(8,128)(2,1)} fusion(bf16[96,768,256]{2,1,0:T(8,128)(2,1)} %bitcast.45, bf16[768,768]{1,0:T(8,128)(2,1)S(1)} %copy-done.1), kind=kOutput, calls=%fused_computation.3 | convolution fusion | flops 29009903616 | bytes 76677120 | tf_op jit(solution)/shard_map/yzx,zk->ykx/dot_general | solution.py:23
  1622.8 34.9 %copy.38 = bf16[96,768,256]{2,0,1:T(8,128)(2,1)} copy(bf16[96,768,256]{2,1,0:T(8,128)(2,1)} %convert_bitcast_fusion.1) | data formatting | bytes 75497472 | tf_op jit(solution)/shard_map/convert_element_type | solution.py:25
  1657.7 0.0 copy-start.2
  1657.7 0.0 copy-start.3
  1657.7 0.0 copy-start.4
  1657.7 7.8 all-to-all-start.3
  1665.5 0.0 copy-done.2
  1665.5 0.0 copy-done.3
  1665.5 0.0 copy-done.4
  1665.5 38.3 %convolution_convert_fusion = bf16[768,96,256]{2,0,1:T(8,128)(2,1)} fusion(bf16[768,96,256]{2,0,1:T(8,128)(2,1)} %bitcast.44, bf16[768,768]{1,0:T(8,128)(2,1)S(1)} %copy-done.2, bf16[768,768]{1,0:T(8,128)(2,1)} %param.9, f32[768]{0:T(1024)S(1)} %copy-done.3, f32[768]{0:T(1024)S(1)} %copy-done.4), kind=kOutput, calls=%fused_computation.4 | convolution fusion | flops 29013442560 | bytes 77862912 | tf_op jit(solution)/shard_map/yzx,yk->kzx/dot_general | solution.py:20
  1703.9 34.9 %copy.33 = bf16[768,96,256]{2,1,0:T(8,128)(2,1)} copy(bf16[768,96,256]{2,0,1:T(8,128)(2,1)} %convolution_convert_fusion) | data formatting | bytes 75497472 | tf_op jit(solution)/shard_map/convert_element_type | solution.py:21
  1738.7 737.8 %all-to-all-done.3 = bf16[96,768,256]{2,0,1:T(8,128)(2,1)} async-done(((bf16[96,768,256]{2,0,1:T(8,128)(2,1)}), bf16[96,768,256]{2,0,1:T(8,128)(2,1)}, u32[]{:S(2)}, u32[]{:S(2)}) %all-to-all-start.3) | async-done | bytes 37748768 | tf_op jit(solution)/shard_map/all_to_all | solution.py:24
  2476.6 10.5 all-to-all-start.1
  2487.1 35.0 %copy.40 = bf16[8,96,96,256]{3,2,1,0:T(8,128)(2,1)} copy(bf16[8,96,96,256]{3,1,2,0:T(8,128)(2,1)} %bitcast.15) | data formatting | bytes 75497472 | tf_op jit(solution)/shard_map/all_to_all | solution.py:24
  2522.0 372.8 %all-to-all-done.1 = bf16[768,96,256]{2,1,0:T(8,128)(2,1)} async-done(((bf16[768,96,256]{2,1,0:T(8,128)(2,1)}), bf16[768,96,256]{2,1,0:T(8,128)(2,1)}, u32[]{:S(2)}, u32[]{:S(2)}) %all-to-all-start.1) | async-done | bytes 37748768 | tf_op jit(solution)/shard_map/all_to_all | solution.py:28
  2894.8 10.7 all-to-all-start.4
  2905.5 47.7 %copy.49 = f32[4,192,96,256]{3,0,2,1:T(4,128)} copy(bf16[4,192,96,256]{3,2,1,0:T(8,128)(2,1)} %bitcast.19) | data formatting | bytes 113246208 | tf_op jit(solution)/shard_map/convert_element_type | solution.py:31
  2953.3 90.1 %reshape.14 = f32[192,96,1024]{2,1,0:T(8,128)} reshape(f32[192,96,4,256]{3,2,1,0:T(4,128)} %bitcast.39) | data formatting | bytes 150994944 | tf_op jit(solution)/shard_map/convert_element_type | solution.py:31
  3043.4 270.0 %all-to-all-done.4 = bf16[768,96,256]{2,1,0:T(8,128)(2,1)} async-done(((bf16[768,96,256]{2,1,0:T(8,128)(2,1)}), bf16[768,96,256]{2,1,0:T(8,128)(2,1)}, u32[]{:S(2)}, u32[]{:S(2)}) %all-to-all-start.4) | async-done | bytes 37748768 | tf_op jit(solution)/shard_map/all_to_all | solution.py:29
  3313.3 35.8 %convert_bitcast_fusion = f32[4,192,12,8,256]{4,3,2,1,0:T(8,128)} fusion(bf16[4,192,96,256]{3,2,1,0:T(8,128)(2,1)} %bitcast.21), kind=kLoop, calls=%fused_computation | loop fusion | flops 18874368 | bytes 113246208
  3349.1 48.9 %copy.47 = f32[4,192,12,8,256]{4,3,0,2,1:T(8,128)} copy(f32[4,192,12,8,256]{4,3,2,1,0:T(8,128)} %convert_bitcast_fusion) | data formatting | bytes 150994944 | tf_op jit(solution)/shard_map/convert_element_type | solution.py:31
  3398.0 0.0 copy-done
  3398.0 73.9 %add_convert_fusion = bf16[192,96,1024]{2,1,0:T(8,128)(2,1)} fusion(f32[192,96,1024]{2,1,0:T(8,128)} %bitcast.23, f32[192,96,1024]{2,1,0:T(8,128)} %reshape.14, bf16[192,96,1024]{2,1,0:T(8,128)(2,1)} %param.7, bf16[1024,1024]{1,0:T(8,128)(2,1)S(1)} %copy-done), kind=kOutput, calls=%fused_computation.2 | convolution fusion | flops 38711328768 | bytes 228589568 | tf_op jit(solution)/shard_map/dot_general | solution.py:9
Async XLA Ops:
  0.0 3398.0 %copy-start = (bf16[1024,1024]{1,0:T(8,128)(2,1)S(1)}, bf16[1024,1024]{1,0:T(8,128)(2,1)}, u32[]{:S(2)}) copy-start(bf16[1024,1024]{1,0:T(8,128)(2,1)} %param.8) | copy-start | bytes 6291460
  1552.2 25.6 copy-start.1
  1657.7 7.8 copy-start.2
  1657.7 7.8 copy-start.3
  1657.7 7.8 copy-start.4
  1657.7 818.9 %all-to-all-start.3 = ((bf16[96,768,256]{2,0,1:T(8,128)(2,1)}), bf16[96,768,256]{2,0,1:T(8,128)(2,1)}, u32[]{:S(2)}, u32[]{:S(2)}) async-start(bf16[96,768,256]{2,0,1:T(8,128)(2,1)} %copy.38), calls=%async_computation.3 | async-start | bytes 75497472 | tf_op jit(solution)/shard_map/all_to_all | solution.py:24
  2476.6 418.2 %all-to-all-start.1 = ((bf16[768,96,256]{2,1,0:T(8,128)(2,1)}), bf16[768,96,256]{2,1,0:T(8,128)(2,1)}, u32[]{:S(2)}, u32[]{:S(2)}) async-start(bf16[768,96,256]{2,1,0:T(8,128)(2,1)} %copy.33), calls=%async_computation.1 | async-start | bytes 75497472 | tf_op jit(solution)/shard_map/all_to_all | solution.py:28
  2894.8 418.5 %all-to-all-start.4 = ((bf16[768,96,256]{2,1,0:T(8,128)(2,1)}), bf16[768,96,256]{2,1,0:T(8,128)(2,1)}, u32[]{:S(2)}, u32[]{:S(2)}) async-start(bf16[768,96,256]{2,1,0:T(8,128)(2,1)} %bitcast.41), calls=%async_computation.4 | async-start | bytes 75497472 | tf_op jit(solution)/shard_map/all_to_all | solution.py:29
where the time goes:
time: 3480 us; the launch traced here: 3470 us
  blocking collectives  1390 us (40%)
  waiting for transfers between devices  1380 us (40%)
  local copies, waits for them, and re-layouts  476 us (14%)
  matrix products  157 us (5%)
  other arithmetic  35.8 us (1%)
    all_to_all x1, blocking collectives, per_device(): lax.all_to_all(pencil_y, 'col', split_axis=0, concat_axis=1, tiled=True)  825 us
    all_to_all x1, waiting for transfers between devices, per_device(): lax.all_to_all(z_full.astype(jnp.bfloat16), 'col', split_axis=1, concat_a...  738 us
    all_to_all x1, blocking collectives, per_device(): lax.all_to_all(scalar_field, 'row', split_axis=2, concat_axis=0, tiled=True)  568 us
    all_to_all x1, waiting for transfers between devices, per_device(): lax.all_to_all(y_term, 'row', split_axis=0, concat_axis=2, tiled=True)  373 us
    all_to_all x1, waiting for transfers between devices, per_device(): lax.all_to_all(z_in_y, 'row', split_axis=0, concat_axis=2, tiled=True)  270 us
    convert_element_type x3, local copies, waits for them, and re-layouts, per_device(): total = x_term + y_back.astype(jnp.float32) + z_back.astype(jnp.float32)  187 us
    all_to_all x2, local copies, waits for them, and re-layouts, per_device(): lax.all_to_all(scalar_field, 'row', split_axis=2, concat_axis=0, tiled=True)  101 us
    dot_general x1, matrix products, x_apply(): product = jnp.dot(flat, x_operator, preferred_element_type=jnp.float32)  73.9 us
  transfers between devices with their start and end apart: 3, of which 3 were waited for; matrix products, arithmetic and copies ran while one was open for 7% of the time, Pallas kernels for 0%

commit v1 on v0

v1 whole, which is shorter than its diff:
```python
import functools
import math

import jax
import jax.numpy as jnp
from jax import lax
from jax.experimental import pallas as pl
from jax.experimental.pallas import tpu as pltpu
from jax.sharding import PartitionSpec as P

VMEM_BYTES = 56 * 1024 * 1024


def z_kernel(operator_ref, field_ref, out_ref):
    parts, rows, depth, width = field_ref.shape
    for row in range(rows):
        planes = field_ref[:, row]
        if depth % 16:
            planes = planes.astype(jnp.float32)
        planes = planes.reshape(parts * depth, width).astype(jnp.bfloat16)
        product = jnp.dot(operator_ref[...], planes, preferred_element_type=jnp.float32)
        out_ref[:, row] = product.reshape(parts, depth, width).astype(jnp.bfloat16)


def z_apply(operator, field, first, count, step):
    parts, rows, depth, width = field.shape
    offset = first // step
    points = parts * depth
    return pl.pallas_call(
        z_kernel,
        grid=(count // step,),
        in_specs=[
            pl.BlockSpec((points, points), lambda i: (0, 0)),
            pl.BlockSpec((parts, step, depth, width), lambda i: (0, i + offset, 0, 0)),
        ],
        out_specs=pl.BlockSpec((parts, step, depth, width), lambda i: (0, i, 0, 0)),
        out_shape=jax.ShapeDtypeStruct((parts, count, depth, width), jnp.bfloat16),
        compiler_params=pltpu.CompilerParams(vmem_limit_bytes=VMEM_BYTES),
        cost_estimate=pl.CostEstimate(
            flops=2 * points * points * count * width,
            bytes_accessed=4 * points * count * width,
            transcendentals=0,
        ),
    )(operator, field)


def total_kernel(slabs, row_ref, operator_ref, field_ref, z_ref, *refs):
    y_refs, out_ref, total = refs[: 2 * slabs], refs[-2], refs[-1]
    parts, rows, depth, width = total.shape
    flat = field_ref[...]
    if depth % 16:
        flat = flat.astype(jnp.float32)
    flat = flat.reshape(parts * rows * depth, width).astype(jnp.bfloat16)
    product = jnp.dot(flat, operator_ref[...], preferred_element_type=jnp.float32)
    total[...] = product.reshape(parts, rows, depth, width) + z_ref[...].astype(jnp.float32)
    share = width // slabs // 2
    for half in range(2):
        for distance in range(slabs):
            first = (2 * (row_ref[0] ^ distance) + half) * share
            lanes = pl.ds(pl.multiple_of(first, share), share)
            total[:, :, :, lanes] += y_refs[half * slabs + distance][...].astype(jnp.float32)
    out_ref[...] = total[...].astype(jnp.bfloat16)


def total_into(so_far, first, step, together, row, operator, field, z_term, y_terms):
    parts, count, depth, width = z_term.shape
    offset = first // step
    share = y_terms[0].shape[3]
    here = pl.BlockSpec((together, step, depth, width), lambda p, i, r: (p, i + offset, 0, 0))
    in_specs = [
        pl.BlockSpec((width, width), lambda p, i, r: (0, 0)),
        here,
        pl.BlockSpec((together, step, depth, width), lambda p, i, r: (p, i, 0, 0)),
    ] + [
        pl.BlockSpec((together, step, depth, share), lambda p, i, r: (p, i + offset, 0, 0))
        for _ in y_terms
    ]
    operands = [operator, field, z_term, *y_terms]
    aliases = {}
    if so_far is not None:
        in_specs.append(pl.BlockSpec(memory_space=pl.ANY))
        operands.append(so_far)
        aliases = {len(operands): 0}
    return pl.pallas_call(
        functools.partial(total_kernel, len(y_terms) // 2),
        grid_spec=pltpu.PrefetchScalarGridSpec(
            num_scalar_prefetch=1,
            grid=(parts // together, count // step),
            in_specs=in_specs,
            out_specs=here,
            scratch_shapes=[pltpu.VMEM((together, step, depth, width), jnp.float32)],
        ),
        out_shape=jax.ShapeDtypeStruct(field.shape, jnp.bfloat16),
        input_output_aliases=aliases,
        compiler_params=pltpu.CompilerParams(vmem_limit_bytes=VMEM_BYTES),
        cost_estimate=pl.CostEstimate(
            flops=2 * width * width * parts * count * depth,
            bytes_accessed=8 * width * parts * count * depth,
            transcendentals=0,
        ),
    )(row, *operands)


def swap(value, axis, size, distance):
    return lax.ppermute(value, axis, [(i, i ^ distance) for i in range(size)])


def chunk_sizes(share):
    end = max(1, share // 12)
    middle = share - 2 * end
    if middle < 2 * end:
        return [share]
    second = (2 * middle // 5) // end * end
    return [end, middle - second, second, end]


def per_device(rows, cols, scalar_field, x_operator, y_second, y_first, y_stretch, y_curve, z_operator):
    ny, nz, nx = scalar_field.shape
    me = lax.axis_index("row")
    y_combined = (
        y_stretch[None, :] * y_second.astype(jnp.float32)
        + y_curve[None, :] * y_first.astype(jnp.float32)
    ).astype(jnp.bfloat16)
    z_transposed = z_operator.T

    share = ny // cols
    planes = lax.all_to_all(scalar_field, "col", 0, 0, tiled=True)

    half = nx // rows // 2
    y_blocks = y_combined.reshape(rows, ny, rows, ny)
    by_distance = jnp.stack([y_blocks[me ^ d] for d in range(rows)])
    by_distance = jnp.stack([by_distance[:, :, me ^ d] for d in range(rows)], axis=2)
    by_distance = by_distance.reshape(rows * ny, rows, ny)

    def y_pencil(side):
        pieces = []
        for d in range(rows):
            first = (2 * (me ^ d) + side) * half
            piece = lax.dynamic_slice_in_dim(scalar_field, first, half, 2)
            pieces.append(piece if d == 0 else swap(piece, "row", rows, d))
        return jnp.concatenate(pieces, axis=0)

    def y_multiply(pencil):
        product = jnp.einsum(
            "yzx,ydk->dkzx", pencil, by_distance, preferred_element_type=jnp.float32
        ).astype(jnp.bfloat16)
        return [product[d] for d in range(rows)]

    def y_return(pieces):
        back = [pieces[d] if d == 0 else swap(pieces[d], "row", rows, d) for d in range(rows)]
        return [value.reshape(cols, share, nz, half) for value in back]

    pencils = [y_pencil(side) for side in range(2)]
    y_first_half, y_second_half = [y_multiply(pencil) for pencil in pencils]
    y_first_half = y_return(y_first_half)
    planes, y_first_half, y_second_half = lax.optimization_barrier(
        (planes, y_first_half, y_second_half)
    )
    y_second_half = y_return(y_second_half)

    planes = planes.reshape(cols, share, nz, nx)
    field = scalar_field.reshape(cols, share, nz, nx)
    where = me.reshape(1).astype(jnp.int32)
    sizes = chunk_sizes(share)
    step = math.gcd(*sizes)
    starts = [sum(sizes[:c]) for c in range(len(sizes))]
    last = len(sizes) - 1

    def z_chunk(c):
        return z_apply(z_transposed, planes, starts[c], sizes[c], step)

    def z_return(product):
        flat = product.reshape(-1, nz, nx)
        return lax.all_to_all(flat, "col", 0, 0, tiled=True).reshape(product.shape)

    def add_chunk(result, c, z_term):
        together = math.gcd(cols, 2 if c == last else 4)
        y_terms = y_first_half + y_second_half
        return total_into(
            result, starts[c], step, together, where, x_operator, field, z_term, y_terms
        )

    z_back, result = [], None
    for c in range(len(sizes)):
        product = z_chunk(c)
        if c == max(last - 1, 0):
            product, y_second_half = lax.optimization_barrier((product, y_second_half))
        if c == last and last >= 2:
            for earlier in range(last - 1):
                result = add_chunk(result, earlier, z_back[earlier])
            product, result = lax.optimization_barrier((product, result))
        z_back.append(z_return(product))
    for c in range(max(last - 1, 0), len(sizes)):
        result = add_chunk(result, c, z_back[c])
    return result.reshape(ny, nz, nx)


def solution(mesh):
    rows, cols = mesh.shape["row"], mesh.shape["col"]
    in_specs = (P("row", "col", None), P(), P(), P(), P(), P(), P())
    return jax.shard_map(
        functools.partial(per_device, rows, cols),
        mesh=mesh,
        in_specs=in_specs,
        out_specs=P("row", "col", None),
        check_vma=False,
    )
```

time: 3480 us -> 1680 us (0.48)
  blocking collectives: 1390 us -> 0 us
  local copies, waits for them, and re-layouts: 476 us -> 168 us
  Pallas kernels: 0 us -> 134 us
  matrix products: 157 us -> 39.8 us
  waiting for transfers between devices: 1380 us -> 1290 us
    all_to_all x2 -> x0, blocking collectives: 1390 us -> none  [the longest x1 825 us: per_device(): lax.all_to_all(pencil_y, 'col', split_axis=0, concat_axis=1, tiled=True)]
    all_to_all x3 -> x5, waiting for transfers between devices: 1380 us -> 655 us  [the longest x4 507 us: z_return(): return lax.all_to_all(flat, 'col', 0, 0, tiled=True).reshape(product.shape)]
    ppermute x0 -> x12, waiting for transfers between devices: none -> 639 us  [swap(): return lax.ppermute(value, axis, [(i, i ^ distance) for i in range(size)])]
    convert_element_type x5 -> x0, local copies, waits for them, and re-layouts: 256 us -> none  [the longest x3 187 us: per_device(): total = x_term + y_back.astype(jnp.float32) + z_back.astype(jnp.float32)]
    all_to_all x4 -> x0, local copies, waits for them, and re-layouts: 161 us -> none  [the longest x2 101 us: per_device(): lax.all_to_all(scalar_field, 'row', split_axis=2, concat_axis=0, tiled=True)]
    pallas_call x0 -> x8, Pallas kernels: none -> 134 us  [the longest x4 85.5 us: total_into(): pl.pallas_call(functools.partial(total_kernel, len(y_terms) // 2), grid_s...]
    dot_general x3 -> x2, matrix products: 157 us -> 39.8 us  [y_multiply(): jnp.einsum('yzx,ydk->dkzx', pencil, by_distance, preferred_element_type=j...]
    ppermute x0 -> x6, local copies, waits for them, and re-layouts: none -> 42.9 us  [swap(): return lax.ppermute(value, axis, [(i, i ^ distance) for i in range(size)])]
  transfers between devices with their start and end apart: 3 -> 17, of which waited for: 3 -> 13; matrix products, arithmetic and copies ran while one was open for 7% -> 13% of each run, Pallas kernels for 0% -> 7%
where the time goes in v1:
time: 1680 us
  waiting for transfers between devices  1290 us (77%)
  local copies, waits for them, and re-layouts  168 us (10%)
  Pallas kernels  134 us (8%)
  matrix products  39.8 us (2%)
  starting transfers between devices  37 us (2%)
    ppermute x12, waiting for transfers between devices, swap(): return lax.ppermute(value, axis, [(i, i ^ distance) for i in range(size)])  639 us
    all_to_all x4, waiting for transfers between devices, z_return(): return lax.all_to_all(flat, 'col', 0, 0, tiled=True).reshape(product.shape)  507 us
    all_to_all x1, waiting for transfers between devices, per_device(): planes = lax.all_to_all(scalar_field, 'col', 0, 0, tiled=True)  148 us
    pallas_call x4, Pallas kernels, total_into(): pl.pallas_call(functools.partial(total_kernel, len(y_terms) // 2), grid_s...  85.5 us
    unnamed x41, local copies, waits for them, and re-layouts  53.5 us
    pallas_call x4, Pallas kernels, z_apply(): pl.pallas_call(z_kernel, grid=(count // step,), in_specs=[pl.BlockSpec((p...  48.8 us
    ppermute x6, local copies, waits for them, and re-layouts, swap(): return lax.ppermute(value, axis, [(i, i ^ distance) for i in range(size)])  42.9 us
    dot_general x2, matrix products, y_multiply(): jnp.einsum('yzx,ydk->dkzx', pencil, by_distance, preferred_element_type=j...  39.8 us
  transfers between devices with their start and end apart: 17, of which 13 were waited for; matrix products, arithmetic and copies ran while one was open for 13% of the time, Pallas kernels for 7%

profile of v1, /device:TPU:0, one launch (start us, length us, event | category | flops | bytes accessed | tf_op | source)
XLA Modules:
  0.0 1680.9 jit_solution(7271714871733567886)
XLA Ops:
  0.0 7.5 all-to-all-start
  7.5 26.6 %constant_dynamic-slice_fusion.3 = (bf16[192,96,128]{2,1,0:T(8,128)(2,1)}, bf16[192,96,128]{2,1,0:T(8,128)(2,1)}, bf16[192,96,128]{2,1,0:T(8,128)(2,1)}, bf16[19...) fusion(bf16[192,96,1024]{2,1,0:T(8,128)(2,1)} %param.7, ...), kind=kLoop, calls=%fused_computation.33 | loop fusion | bytes 75497504 | tf_op jit(solution)/shard_map/dynamic_slice | solution.py:139
  34.2 6.4 copy.38
  41.0 6.4 copy.39
  47.5 2.5 collective-permute-start.1
  50.0 4.0 copy.40
  54.1 4.0 copy.44
  58.0 1.6 collective-permute-start.8
  59.7 4.0 copy.42
  63.9 1.7 add_convert_fusion
  65.6 1.4 reshape.67
  67.0 0.6 constant_dynamic-slice_fusion.15
  67.6 1.9 copy.33
  69.5 1.7 copy.35
  71.2 1.7 copy.34
  72.9 1.7 copy.36
  74.6 6.3 copy.43
  80.9 4.1 pad_maximum_fusion
  85.9 1.5 pad_maximum_fusion.1
  87.5 1.4 reshape.86
  88.9 4.2 copy.37
  93.1 59.9 %collective-permute-done.1 = bf16[192,96,128]{2,0,1:T(8,128)(2,1)} collective-permute-done((bf16[192,96,128]{2,0,1:T(8,128)(2,1)}, bf16[192,96,128]{2,0,1:T(8,128)(2,1)}, u32[]{:S(2)}, u32[]{:S(2)}) %collective-permute-start.1) | collective-permute-done | bytes 4718624 | tf_op jit(solution)/shard_map/ppermute | solution.py:105
  152.9 100.8 %collective-permute-done.2 = bf16[192,96,128]{2,0,1:T(8,128)(2,1)} collective-permute-done((bf16[192,96,128]{2,0,1:T(8,128)(2,1)}, bf16[192,96,128]{2,0,1:T(8,128)(2,1)}, u32[]{:S(2)}, u32[]{:S(2)}) %collective-permute-start.2) | collective-permute-done | bytes 4718624 | tf_op jit(solution)/shard_map/ppermute | solution.py:105
  253.7 19.6 %fusion.15 = bf16[4,192,96,128]{3,1,2,0:T(8,128)(2,1)} fusion(bf16[192,96,128]{2,0,1:T(8,128)(2,1)} %collective-permute-done.2, bf16[192,96,128]{2,0,1:T(8,128)(2,1)} %collective-permute-done.1, bf16[192,96,128]{2,0,1:T(8,128)(2,1)} %collective-permute-done, bf16[192,96,128]{2,0,1:T(8,128)(2,1)S(1)} %copy.37, bf16[768,4,192,1]{0,2,1,3:T(8,128)(2,1)S(1)} %reshape.86), kind=kOutput, calls=%fused_computation.17 | convolution fusion | flops 14580449280 | bytes 38928384 | tf_op jit(solution)/shard_map/yzx,ydk->dkzx/dot_general | solution.py:144
  273.3 14.1 slice_bitcast_fusion.4
  287.4 2.0 collective-permute-start.5
  289.5 65.3 %collective-permute-done.8 = bf16[192,96,128]{2,0,1:T(8,128)(2,1)} collective-permute-done((bf16[192,96,128]{2,0,1:T(8,128)(2,1)}, bf16[192,96,128]{2,0,1:T(8,128)(2,1)}, u32[]{:S(2)}, u32[]{:S(2)}) %collective-permute-start.8) | collective-permute-done | bytes 4718624 | tf_op jit(solution)/shard_map/ppermute | solution.py:105
  355.3 1.5 copy.11
  356.7 6.5 copy.41
  363.3 5.2 copy.20
  368.5 87.8 %collective-permute-done.7 = bf16[192,96,128]{2,0,1:T(8,128)(2,1)} collective-permute-done((bf16[192,96,128]{2,0,1:T(8,128)(2,1)}, bf16[192,96,128]{2,0,1:T(8,128)(2,1)}, u32[]{:S(2)}, u32[]{:S(2)}) %collective-permute-start.7) | collective-permute-done | bytes 4718624 | tf_op jit(solution)/shard_map/ppermute | solution.py:105
  456.3 20.1 %fusion.14 = bf16[4,192,96,128]{3,1,2,0:T(8,128)(2,1)} fusion(bf16[192,96,128]{2,0,1:T(8,128)(2,1)} %collective-permute-done.8, bf16[192,96,128]{2,0,1:T(8,128)(2,1)} %collective-permute-done.7, bf16[192,96,128]{2,0,1:T(8,128)(2,1)} %collective-permute-done.6, bf16[192,96,128]{2,0,1:T(8,128)(2,1)} %copy.41, bf16[768,4,192,1]{0,2,1,3:T(8,128)(2,1)S(1)} %reshape.86), kind=kOutput, calls=%fused_computation.16 | convolution fusion | flops 14580449280 | bytes 38928384 | tf_op jit(solution)/shard_map/yzx,ydk->dkzx/dot_general | solution.py:144
  476.4 14.2 slice_bitcast_fusion
  490.6 66.4 %collective-permute-done.5 = bf16[192,96,128]{2,0,1:T(8,128)(2,1)} collective-permute-done((bf16[192,96,128]{2,0,1:T(8,128)(2,1)}, bf16[192,96,128]{2,0,1:T(8,128)(2,1)}, u32[]{:S(2)}, u32[]{:S(2)}) %collective-permute-start.5) | collective-permute-done | bytes 4718624 | tf_op jit(solution)/shard_map/ppermute | solution.py:105
  557.0 7.5 copy.23
  564.5 93.8 %collective-permute-done.4 = bf16[192,96,128]{2,0,1:T(8,128)(2,1)} collective-permute-done((bf16[192,96,128]{2,0,1:T(8,128)(2,1)}, bf16[192,96,128]{2,0,1:T(8,128)(2,1)}, u32[]{:S(2)}, u32[]{:S(2)}) %collective-permute-start.4) | collective-permute-done | bytes 4718624 | tf_op jit(solution)/shard_map/ppermute | solution.py:105
  658.3 7.5 copy.22
  665.8 7.5 copy.21
  673.4 148.2 %all-to-all-done = bf16[192,96,1024]{2,1,0:T(8,128)(2,1)} async-done(((bf16[192,96,1024]{2,1,0:T(8,128)(2,1)}), bf16[192,96,1024]{2,1,0:T(8,128)(2,1)}, u32[]{:S(2)}, u32[]{:S(2)}) %all-to-all-start) | async-done | bytes 37748768 | tf_op jit(solution)/shard_map/all_to_all | solution.py:127
  821.6 6.5 shard_map.76
  828.1 3.8 all-to-all-start.2
  831.9 20.6 %shard_map.74 = bf16[8,12,96,1024]{3,2,1,0:T(8,128)(2,1)} custom-call(bf16[768,768]{1,0:T(8,128)(2,1)} %bitcast.91, bf16[8,24,96,1024]{3,2,1,0:T(8,128)(2,1)} %bitcast.17.field_ref), custom_call_target="tpu_custom_call" | custom-call | flops 14495514624 | bytes 37748736 | tf_op jit(solution)/shard_map/pallas_call | solution.py:29
  852.6 50.0 %all-to-all-done.2 = bf16[16,96,1024]{2,1,0:T(8,128)(2,1)S(1)} async-done(((bf16[16,96,1024]{2,1,0:T(8,128)(2,1)}), bf16[16,96,1024]{2,1,0:T(8,128)(2,1)S(1)}, u32[]{:S(2)}, u32[]{:S(2)}) %all-to-all-start.2) | async-done | bytes 3145760 | tf_op jit(solution)/shard_map/all_to_all | solution.py:174
  902.6 1.6 copy-done
  904.2 5.9 all-to-all-start.1
  910.2 1.6 collective-permute-start.10
  912.1 7.5 copy.28
  919.6 15.1 shard_map.75
  934.6 7.6 copy.29
  942.3 72.9 %collective-permute-done.10 = bf16[192,96,128]{2,0,1:T(8,128)(2,1)} collective-permute-done((bf16[192,96,128]{2,0,1:T(8,128)(2,1)}, bf16[192,96,128]{2,0,1:T(8,128)(2,1)}, u32[]{:S(2)}, u32[]{:S(2)}) %collective-permute-start.10) | collective-permute-done | bytes 4718624 | tf_op jit(solution)/shard_map/ppermute | solution.py:105
  1015.2 7.6 copy.30
  1022.8 92.5 %collective-permute-done.11 = bf16[192,96,128]{2,0,1:T(8,128)(2,1)S(1)} collective-permute-done((bf16[192,96,128]{2,0,1:T(8,128)(2,1)}, bf16[192,96,128]{2,0,1:T(8,128)(2,1)S(1)}, u32[]{:S(2)}, u32[]{:S(2)}) %collective-permute-start.11) | collective-permute-done | bytes 4718624 | tf_op jit(solution)/shard_map/ppermute | solution.py:105
  1115.3 5.2 copy.31
  1120.4 196.6 %all-to-all-done.1 = bf16[96,96,1024]{2,1,0:T(8,128)(2,1)} async-done(((bf16[96,96,1024]{2,1,0:T(8,128)(2,1)}), bf16[96,96,1024]{2,1,0:T(8,128)(2,1)}, u32[]{:S(2)}, u32[]{:S(2)}) %all-to-all-start.1) | async-done | bytes 18874400 | tf_op jit(solution)/shard_map/all_to_all | solution.py:174
  1317.1 5.6 all-to-all-start.4
  1322.7 6.5 shard_map.73
  1329.2 9.8 shard_map.77.refs_8_
  1339.0 38.8 %shard_map.78.refs_8_ = bf16[8,24,96,1024]{3,2,1,0:T(8,128)(2,1)} custom-call(s32[1]{0:T(128)} %bitcast.row_ref, bf16[1024,1024]{1,0:T(8,128)(2,1)} %operator_ref.7, bf16[8,24,96,1024]{3,2,1,0:T(8,128)(2,1)} %bitcast.53, bf16[8,12,96,1024]{3,2,1,0:T(8,128)(2,1)} %bitcast.19.z_ref, ...), custom_call_target="tpu_custom_call", output_to_operand_aliasing={{}: (12, {})} | custom-call | flops 19327352832 | bytes 75497472 | tf_op jit(solution)/shard_map/pallas_call | solution.py:84
  1377.8 216.3 %all-to-all-done.4 = bf16[64,96,1024]{2,1,0:T(8,128)(2,1)} async-done(((bf16[64,96,1024]{2,1,0:T(8,128)(2,1)}), bf16[64,96,1024]{2,1,0:T(8,128)(2,1)}, u32[]{:S(2)}, u32[]{:S(2)}) %all-to-all-start.4) | async-done | bytes 12582944 | tf_op jit(solution)/shard_map/all_to_all | solution.py:174
  1594.1 4.3 all-to-all-start.3
  1598.5 27.2 %shard_map.79.refs_8_ = bf16[8,24,96,1024]{3,2,1,0:T(8,128)(2,1)} custom-call(s32[1]{0:T(128)} %bitcast.row_ref, bf16[1024,1024]{1,0:T(8,128)(2,1)} %operator_ref.7, bf16[8,24,96,1024]{3,2,1,0:T(8,128)(2,1)} %bitcast.54, bf16[8,8,96,1024]{3,2,1,0:T(8,128)(2,1)} %bitcast.29.z_ref, bf16[8,24,96,128]{3,2,1,0:T(8,128)(2,1)} %bitcast.58, ...), custom_call_target="tpu_custom_call", output_to_operand_aliasing={{}: (12, {})} | custom-call | flops 12884901888 | bytes 50331648 | tf_op jit(solution)/shard_map/pallas_call | solution.py:84
  1625.7 43.7 %all-to-all-done.3 = bf16[16,96,1024]{2,1,0:T(8,128)(2,1)S(1)} async-done(((bf16[16,96,1024]{2,1,0:T(8,128)(2,1)}), bf16[16,96,1024]{2,1,0:T(8,128)(2,1)S(1)}, u32[]{:S(2)}, u32[]{:S(2)}) %all-to-all-start.3) | async-done | bytes 3145760 | tf_op jit(solution)/shard_map/all_to_all | solution.py:174
  1669.4 1.6 copy-done.1
  1671.0 9.6 shard_map.80
  (43 shorter events, 2.7 us)
Async XLA Ops:
  0.0 821.6 %all-to-all-start = ((bf16[192,96,1024]{2,1,0:T(8,128)(2,1)}), bf16[192,96,1024]{2,1,0:T(8,128)(2,1)}, u32[]{:S(2)}, u32[]{:S(2)}) async-start(bf16[192,96,1024]{2,1,0:T(8,128)(2,1)} %param.7), calls=%async_computation | async-start | bytes 75497472 | tf_op jit(solution)/shard_map/all_to_all | solution.py:127
  34.1 15.8 slice-start.4
  34.2 19.9 %slice-start.2 = ((s8[4718592]{0:T(1024)(128)(4,1)}), s8[4194304]{0:T(1024)(128)(4,1)S(1)}, s32[]{:S(2)}) async-start(s8[4718592]{0:T(1024)(128)(4,1)} %bitcast.96), calls=%async_computation.7 | async-start | bytes 8388608
  40.6 45.0 %collective-permute-start = (bf16[192,96,128]{2,0,1:T(8,128)(2,1)}, bf16[192,96,128]{2,0,1:T(8,128)(2,1)}, u32[]{:S(2)}, u32[]{:S(2)}) collective-permute-start(bf16[192,96,128]{2,0,1:T(8,128)(2,1)} %copy.38), channel_id=1, source_target_pairs={{0,8},{8,0},{16,24},{24,16},{1,9},{9,1},{17,25},{25,17},{2,10},{10... | collective-permute-start | bytes 14155784 | tf_op jit(solution)/shard_map/ppermute | solution.py:105
  41.0 8.9 slice-start.5
  41.0 13.0 slice-start.3
  47.5 105.5 %collective-permute-start.1 = (bf16[192,96,128]{2,0,1:T(8,128)(2,1)}, bf16[192,96,128]{2,0,1:T(8,128)(2,1)}, u32[]{:S(2)}, u32[]{:S(2)}) collective-permute-start(bf16[192,96,128]{2,0,1:T(8,128)(2,1)} %copy.39), channel_id=1, source_target_pairs={{0,16},{8,24},{16,0},{24,8},{1,17},{9,25},{17,1},{25,9},{2,18},{10... | collective-permute-start | bytes 14155784 | tf_op jit(solution)/shard_map/ppermute | solution.py:105
  50.0 9.7 slice-start
  53.9 199.7 %collective-permute-start.2 = (bf16[192,96,128]{2,0,1:T(8,128)(2,1)}, bf16[192,96,128]{2,0,1:T(8,128)(2,1)}, u32[]{:S(2)}, u32[]{:S(2)}) collective-permute-start(bf16[192,96,128]{2,0,1:T(8,128)(2,1)} %copy.40), channel_id=1, source_target_pairs={{0,24},{8,16},{16,8},{24,0},{1,25},{9,17},{17,9},{25,1},{2,26},{10... | collective-permute-start | bytes 14155784 | tf_op jit(solution)/shard_map/ppermute | solution.py:105
  54.1 5.6 slice-start.1
  58.0 296.8 %collective-permute-start.8 = (bf16[192,96,128]{2,0,1:T(8,128)(2,1)}, bf16[192,96,128]{2,0,1:T(8,128)(2,1)}, u32[]{:S(2)}, u32[]{:S(2)}) collective-permute-start(bf16[192,96,128]{2,0,1:T(8,128)(2,1)} %copy.44), channel_id=1, source_target_pairs={{0,24},{8,16},{16,8},{24,0},{1,25},{9,17},{17,9},{25,1},{2,26},{10... | collective-permute-start | bytes 14155784 | tf_op jit(solution)/shard_map/ppermute | solution.py:105
  59.6 4.2 copy-start.2
  59.7 4.2 copy-start.4
  59.7 4.2 copy-start.5
  63.7 304.8 %collective-permute-start.6 = (bf16[192,96,128]{2,0,1:T(8,128)(2,1)}, bf16[192,96,128]{2,0,1:T(8,128)(2,1)}, u32[]{:S(2)}, u32[]{:S(2)}) collective-permute-start(bf16[192,96,128]{2,0,1:T(8,128)(2,1)} %copy.42), channel_id=1, source_target_pairs={{0,8},{8,0},{16,24},{24,16},{1,9},{9,1},{17,25},{25,17},{2,10},{10... | collective-permute-start | bytes 14155784 | tf_op jit(solution)/shard_map/ppermute | solution.py:105
  85.6 370.7 %collective-permute-start.7 = (bf16[192,96,128]{2,0,1:T(8,128)(2,1)}, bf16[192,96,128]{2,0,1:T(8,128)(2,1)}, u32[]{:S(2)}, u32[]{:S(2)}) collective-permute-start(bf16[192,96,128]{2,0,1:T(8,128)(2,1)} %copy.43), channel_id=1, source_target_pairs={{0,16},{8,24},{16,0},{24,8},{1,17},{9,25},{17,1},{25,9},{2,18},{10... | collective-permute-start | bytes 14155784 | tf_op jit(solution)/shard_map/ppermute | solution.py:105
  273.3 82.0 %copy-start.3 = (bf16[768,768]{1,0:T(8,128)(2,1)S(1)}, bf16[768,768]{1,0:T(8,128)(2,1)}, u32[]{:S(2)}) copy-start(bf16[768,768]{1,0:T(8,128)(2,1)} %param.13) | copy-start | bytes 3538948
  287.4 269.7 %collective-permute-start.5 = (bf16[192,96,128]{2,0,1:T(8,128)(2,1)}, bf16[192,96,128]{2,0,1:T(8,128)(2,1)}, u32[]{:S(2)}, u32[]{:S(2)}) collective-permute-start(bf16[192,96,128]{2,0,1:T(8,128)(2,1)} %get-tuple-element.49), channel_id=1, source_target_pairs={{0,24},{8,16},{16,8},{24,0},{1,25},{9,17},{17,9},{25,1},{2,26},{10... | collective-permute-start | bytes 14155784 | tf_op jit(solution)/shard_map/ppermute | solution.py:105
  289.4 368.9 %collective-permute-start.4 = (bf16[192,96,128]{2,0,1:T(8,128)(2,1)}, bf16[192,96,128]{2,0,1:T(8,128)(2,1)}, u32[]{:S(2)}, u32[]{:S(2)}) collective-permute-start(bf16[192,96,128]{2,0,1:T(8,128)(2,1)} %get-tuple-element.50), channel_id=1, source_target_pairs={{0,16},{8,24},{16,0},{24,8},{1,17},{9,25},{17,1},{25,9},{2,18},{10... | collective-permute-start | bytes 14155784 | tf_op jit(solution)/shard_map/ppermute | solution.py:105
  354.8 311.0 %collective-permute-start.3 = (bf16[192,96,128]{2,0,1:T(8,128)(2,1)}, bf16[192,96,128]{2,0,1:T(8,128)(2,1)}, u32[]{:S(2)}, u32[]{:S(2)}) collective-permute-start(bf16[192,96,128]{2,0,1:T(8,128)(2,1)} %get-tuple-element.51), channel_id=1, source_target_pairs={{0,8},{8,0},{16,24},{24,16},{1,9},{9,1},{17,25},{25,17},{2,10},{10... | collective-permute-start | bytes 14155784 | tf_op jit(solution)/shard_map/ppermute | solution.py:105
  355.3 8.0 slice-start.6
  356.7 6.5 slice-start.7
  828.1 74.5 %all-to-all-start.2 = ((bf16[16,96,1024]{2,1,0:T(8,128)(2,1)}), bf16[16,96,1024]{2,1,0:T(8,128)(2,1)S(1)}, u32[]{:S(2)}, u32[]{:S(2)}) async-start(bf16[16,96,1024]{2,1,0:T(8,128)(2,1)} %bitcast.102), calls=%async_computation.2 | async-start | bytes 6291456 | tf_op jit(solution)/shard_map/all_to_all | solution.py:174
  902.6 1.6 copy-start
  904.2 412.9 %all-to-all-start.1 = ((bf16[96,96,1024]{2,1,0:T(8,128)(2,1)}), bf16[96,96,1024]{2,1,0:T(8,128)(2,1)}, u32[]{:S(2)}, u32[]{:S(2)}) async-start(bf16[96,96,1024]{2,1,0:T(8,128)(2,1)} %bitcast.88), calls=%async_computation.1 | async-start | bytes 37748736 | tf_op jit(solution)/shard_map/all_to_all | solution.py:174
  910.1 24.5 %collective-permute-start.9 = (bf16[192,96,128]{2,0,1:T(8,128)(2,1)}, bf16[192,96,128]{2,0,1:T(8,128)(2,1)}, u32[]{:S(2)}, u32[]{:S(2)}) collective-permute-start(bf16[192,96,128]{2,0,1:T(8,128)(2,1)} %get-tuple-element.27), channel_id=1, source_target_pairs={{0,8},{8,0},{16,24},{24,16},{1,9},{9,1},{17,25},{25,17},{2,10},{10... | collective-permute-start | bytes 14155784 | tf_op jit(solution)/shard_map/ppermute | solution.py:105
  910.2 105.0 %collective-permute-start.10 = (bf16[192,96,128]{2,0,1:T(8,128)(2,1)}, bf16[192,96,128]{2,0,1:T(8,128)(2,1)}, u32[]{:S(2)}, u32[]{:S(2)}) collective-permute-start(bf16[192,96,128]{2,0,1:T(8,128)(2,1)} %get-tuple-element.28), channel_id=1, source_target_pairs={{0,16},{8,24},{16,0},{24,8},{1,17},{9,25},{17,1},{25,9},{2,18},{10... | collective-permute-start | bytes 14155784 | tf_op jit(solution)/shard_map/ppermute | solution.py:105
  911.8 203.5 %collective-permute-start.11 = (bf16[192,96,128]{2,0,1:T(8,128)(2,1)}, bf16[192,96,128]{2,0,1:T(8,128)(2,1)S(1)}, u32[]{:S(2)}, u32[]{:S(2)}) collective-permute-start(bf16[192,96,128]{2,0,1:T(8,128)(2,1)} %get-tuple-element.29), channel_id=1, source_target_pairs={{0,24},{8,16},{16,8},{24,0},{1,25},{9,17},{17,9},{25,1},{2,26},{10... | collective-permute-start | bytes 14155784 | tf_op jit(solution)/shard_map/ppermute | solution.py:105
  1317.1 277.1 %all-to-all-start.4 = ((bf16[64,96,1024]{2,1,0:T(8,128)(2,1)}), bf16[64,96,1024]{2,1,0:T(8,128)(2,1)}, u32[]{:S(2)}, u32[]{:S(2)}) async-start(bf16[64,96,1024]{2,1,0:T(8,128)(2,1)} %bitcast.89), calls=%async_computation.4 | async-start | bytes 25165824 | tf_op jit(solution)/shard_map/all_to_all | solution.py:174
  1594.1 75.2 %all-to-all-start.3 = ((bf16[16,96,1024]{2,1,0:T(8,128)(2,1)}), bf16[16,96,1024]{2,1,0:T(8,128)(2,1)S(1)}, u32[]{:S(2)}, u32[]{:S(2)}) async-start(bf16[16,96,1024]{2,1,0:T(8,128)(2,1)} %bitcast.26), calls=%async_computation.3 | async-start | bytes 6291456 | tf_op jit(solution)/shard_map/all_to_all | solution.py:174
  1669.4 1.6 copy-start.1

commit v2 on v1

--- a/solution.py
+++ b/solution.py
@@ -22,18 +22,17 @@
         out_ref[:, row] = product.reshape(parts, depth, width).astype(jnp.bfloat16)
 
 
-def z_apply(operator, field, first, count, step):
+def z_apply(operator, field, first, count):
     parts, rows, depth, width = field.shape
-    offset = first // step
     points = parts * depth
     return pl.pallas_call(
         z_kernel,
-        grid=(count // step,),
+        grid=(count,),
         in_specs=[
             pl.BlockSpec((points, points), lambda i: (0, 0)),
-            pl.BlockSpec((parts, step, depth, width), lambda i: (0, i + offset, 0, 0)),
+            pl.BlockSpec((parts, 1, depth, width), lambda i: (0, i + first, 0, 0)),
         ],
-        out_specs=pl.BlockSpec((parts, step, depth, width), lambda i: (0, i, 0, 0)),
+        out_specs=pl.BlockSpec((parts, 1, depth, width), lambda i: (0, i, 0, 0)),
         out_shape=jax.ShapeDtypeStruct((parts, count, depth, width), jnp.bfloat16),
         compiler_params=pltpu.CompilerParams(vmem_limit_bytes=VMEM_BYTES),
         cost_estimate=pl.CostEstimate(
@@ -45,34 +44,41 @@
 
 
 def total_kernel(slabs, row_ref, operator_ref, field_ref, z_ref, *refs):
-    y_refs, out_ref, total = refs[: 2 * slabs], refs[-2], refs[-1]
-    parts, rows, depth, width = total.shape
-    flat = field_ref[...]
-    if depth % 16:
-        flat = flat.astype(jnp.float32)
-    flat = flat.reshape(parts * rows * depth, width).astype(jnp.bfloat16)
-    product = jnp.dot(flat, operator_ref[...], preferred_element_type=jnp.float32)
-    total[...] = product.reshape(parts, rows, depth, width) + z_ref[...].astype(jnp.float32)
-    share = width // slabs // 2
-    for half in range(2):
-        for distance in range(slabs):
-            first = (2 * (row_ref[0] ^ distance) + half) * share
-            lanes = pl.ds(pl.multiple_of(first, share), share)
-            total[:, :, :, lanes] += y_refs[half * slabs + distance][...].astype(jnp.float32)
-    out_ref[...] = total[...].astype(jnp.bfloat16)
-
-
-def total_into(so_far, first, step, together, row, operator, field, z_term, y_terms):
+    y_refs, out_ref = refs[: 2 * slabs], refs[-1]
+    parts, rows, depth, width = out_ref.shape
+    slab = width // slabs
+    share = slab // 2
+
+    def add_all(me):
+        flat = field_ref[...]
+        if depth % 16:
+            flat = flat.astype(jnp.float32)
+        flat = flat.reshape(parts * rows * depth, width).astype(jnp.bfloat16)
+        for owner in range(slabs):
+            lanes = slice(owner * slab, (owner + 1) * slab)
+            product = jnp.dot(flat, operator_ref[:, lanes], preferred_element_type=jnp.float32)
+            product = product.reshape(parts, rows, depth, slab)
+            for half in range(2):
+                here = slice(owner * slab + half * share, owner * slab + (half + 1) * share)
+                y_term = y_refs[half * slabs + (owner ^ me)][...].astype(jnp.float32)
+                z_term = z_ref[:, :, :, here].astype(jnp.float32)
+                x_term = product[:, :, :, half * share : (half + 1) * share]
+                out_ref[:, :, :, here] = (x_term + y_term + z_term).astype(jnp.bfloat16)
+
+    for me in range(slabs):
+        pl.when(row_ref[0] == me)(functools.partial(add_all, me))
+
+
+def total_into(so_far, first, together, row, operator, field, z_term, y_terms):
     parts, count, depth, width = z_term.shape
-    offset = first // step
     share = y_terms[0].shape[3]
-    here = pl.BlockSpec((together, step, depth, width), lambda p, i, r: (p, i + offset, 0, 0))
+    here = pl.BlockSpec((together, 1, depth, width), lambda p, i, r: (p, i + first, 0, 0))
     in_specs = [
         pl.BlockSpec((width, width), lambda p, i, r: (0, 0)),
         here,
-        pl.BlockSpec((together, step, depth, width), lambda p, i, r: (p, i, 0, 0)),
+        pl.BlockSpec((together, 1, depth, width), lambda p, i, r: (p, i, 0, 0)),
     ] + [
-        pl.BlockSpec((together, step, depth, share), lambda p, i, r: (p, i + offset, 0, 0))
+        pl.BlockSpec((together, 1, depth, share), lambda p, i, r: (p, i + first, 0, 0))
         for _ in y_terms
     ]
     operands = [operator, field, z_term, *y_terms]
@@ -85,14 +91,13 @@
         functools.partial(total_kernel, len(y_terms) // 2),
         grid_spec=pltpu.PrefetchScalarGridSpec(
             num_scalar_prefetch=1,
-            grid=(parts // together, count // step),
+            grid=(parts // together, count),
             in_specs=in_specs,
             out_specs=here,
-            scratch_shapes=[pltpu.VMEM((together, step, depth, width), jnp.float32)],
         ),
         out_shape=jax.ShapeDtypeStruct(field.shape, jnp.bfloat16),
         input_output_aliases=aliases,
-        compiler_params=pltpu.CompilerParams(vmem_limit_bytes=VMEM_BYTES),
+        compiler_params=pltpu.CompilerParams(vmem_limit_bytes=VMEM_BYTES // 2),
         cost_estimate=pl.CostEstimate(
             flops=2 * width * width * parts * count * depth,
             bytes_accessed=8 * width * parts * count * depth,
@@ -106,12 +111,10 @@
 
 
 def chunk_sizes(share):
-    end = max(1, share // 12)
-    middle = share - 2 * end
-    if middle < 2 * end:
+    if share < 3:
         return [share]
-    second = (2 * middle // 5) // end * end
-    return [end, middle - second, second, end]
+    last = 2 if share >= 12 else 1
+    return [1, share - 1 - last, last]
 
 
 def per_device(rows, cols, scalar_field, x_operator, y_second, y_first, y_stretch, y_curve, z_operator):
@@ -162,36 +165,32 @@
     field = scalar_field.reshape(cols, share, nz, nx)
     where = me.reshape(1).astype(jnp.int32)
     sizes = chunk_sizes(share)
-    step = math.gcd(*sizes)
     starts = [sum(sizes[:c]) for c in range(len(sizes))]
     last = len(sizes) - 1
-
-    def z_chunk(c):
-        return z_apply(z_transposed, planes, starts[c], sizes[c], step)
 
     def z_return(product):
         flat = product.reshape(-1, nz, nx)
         return lax.all_to_all(flat, "col", 0, 0, tiled=True).reshape(product.shape)
 
-    def add_chunk(result, c, z_term):
-        together = math.gcd(cols, 2 if c == last else 4)
+    def add_chunk(result, c):
+        together = math.gcd(cols, 4 if c == last else 8)
         y_terms = y_first_half + y_second_half
         return total_into(
-            result, starts[c], step, together, where, x_operator, field, z_term, y_terms
+            result, starts[c], together, where, x_operator, field, z_back[c], y_terms
         )
 
     z_back, result = [], None
     for c in range(len(sizes)):
-        product = z_chunk(c)
-        if c == max(last - 1, 0):
-            product, y_second_half = lax.optimization_barrier((product, y_second_half))
-        if c == last and last >= 2:
+        product = z_apply(z_transposed, planes, starts[c], sizes[c])
+        if c == last and last > 0:
             for earlier in range(last - 1):
-                result = add_chunk(result, earlier, z_back[earlier])
+                result = add_chunk(result, earlier)
             product, result = lax.optimization_barrier((product, result))
+        elif c > 0:
+            product, z_back[c - 1] = lax.optimization_barrier((product, z_back[c - 1]))
         z_back.append(z_return(product))
     for c in range(max(last - 1, 0), len(sizes)):
-        result = add_chunk(result, c, z_back[c])
+        result = add_chunk(result, c)
     return result.reshape(ny, nz, nx)
 
 

time: 1680 us -> 1680 us (level)
  Pallas kernels: 134 us -> 112 us
  local copies, waits for them, and re-layouts: 168 us -> 189 us
    pallas_call x4 -> x3, Pallas kernels: 85.5 us -> 63.5 us  [total_into(): pl.pallas_call(functools.partial(total_kernel, len(y_terms) // 2), grid_s...]
    unnamed x41 -> x77, local copies, waits for them, and re-layouts: 53.5 us -> 72.4 us
    all_to_all x4 -> x3, waiting for transfers between devices: 507 us -> 501 us  [z_return(): return lax.all_to_all(flat, 'col', 0, 0, tiled=True).reshape(product.shape)]
    pallas_call x4 -> x3, Pallas kernels: 48.8 us -> 49 us  [z_apply(): pl.pallas_call(z_kernel, grid=(count,), in_specs=[pl.BlockSpec((points, p...]
  transfers between devices with their start and end apart: 17 -> 16, of which waited for: 13 -> 11; matrix products, arithmetic and copies ran while one was open for 13% -> 13% of each run, Pallas kernels for 7% -> 6%
where the time goes in v2:
time: 1680 us
  waiting for transfers between devices  1300 us (77%)
  local copies, waits for them, and re-layouts  189 us (11%)
  Pallas kernels  112 us (7%)
  matrix products  39.8 us (2%)
  starting transfers between devices  32.6 us (2%)
    ppermute x12, waiting for transfers between devices, swap(): return lax.ppermute(value, axis, [(i, i ^ distance) for i in range(size)])  648 us
    all_to_all x3, waiting for transfers between devices, z_return(): return lax.all_to_all(flat, 'col', 0, 0, tiled=True).reshape(product.shape)  501 us
    all_to_all x1, waiting for transfers between devices, per_device(): planes = lax.all_to_all(scalar_field, 'col', 0, 0, tiled=True)  148 us
    unnamed x77, local copies, waits for them, and re-layouts  72.4 us
    pallas_call x3, Pallas kernels, total_into(): pl.pallas_call(functools.partial(total_kernel, len(y_terms) // 2), grid_s...  63.5 us
    pallas_call x3, Pallas kernels, z_apply(): pl.pallas_call(z_kernel, grid=(count,), in_specs=[pl.BlockSpec((points, p...  49 us
    ppermute x6, local copies, waits for them, and re-layouts, swap(): return lax.ppermute(value, axis, [(i, i ^ distance) for i in range(size)])  45.3 us
    dot_general x2, matrix products, y_multiply(): jnp.einsum('yzx,ydk->dkzx', pencil, by_distance, preferred_element_type=j...  39.8 us
  transfers between devices with their start and end apart: 16, of which 11 were waited for; matrix products, arithmetic and copies ran while one was open for 13% of the time, Pallas kernels for 6%

profile of v2, /device:TPU:0, one launch (start us, length us, event | category | flops | bytes accessed | tf_op | source)
XLA Modules:
  0.0 1679.6 jit_solution(1856542958226141102)
XLA Ops:
  0.0 7.5 all-to-all-start
  7.5 26.3 %constant_dynamic-slice_fusion.3 = (bf16[192,96,128]{2,1,0:T(8,128)(2,1)}, bf16[192,96,128]{2,1,0:T(8,128)(2,1)}, bf16[192,96,128]{2,1,0:T(8,128)(2,1)}, bf16[19...) fusion(bf16[192,96,1024]{2,1,0:T(8,128)(2,1)} %param.7, ...), kind=kLoop, calls=%fused_computation.33 | loop fusion | bytes 75497504 | tf_op jit(solution)/shard_map/dynamic_slice | solution.py:142
  33.8 6.5 copy.37
  40.8 6.4 copy.38
  47.2 2.5 collective-permute-start.1
  49.7 4.0 copy.39
  53.8 3.9 copy.43
  57.7 1.6 collective-permute-start.8
  59.4 3.9 copy.41
  63.6 1.7 add_convert_fusion
  67.3 1.9 copy.32
  69.2 1.7 copy.34
  70.9 1.7 copy.33
  72.6 1.7 copy.35
  74.4 6.3 copy.42
  80.6 4.1 pad_maximum_fusion
  85.7 1.5 pad_maximum_fusion.1
  87.2 1.4 reshape.78
  88.6 4.2 copy.36
  92.8 59.8 %collective-permute-done.1 = bf16[192,96,128]{2,0,1:T(8,128)(2,1)} collective-permute-done((bf16[192,96,128]{2,0,1:T(8,128)(2,1)}, bf16[192,96,128]{2,0,1:T(8,128)(2,1)}, u32[]{:S(2)}, u32[]{:S(2)}) %collective-permute-start.1) | collective-permute-done | bytes 4718624 | tf_op jit(solution)/shard_map/ppermute | solution.py:110
  152.6 100.8 %collective-permute-done.2 = bf16[192,96,128]{2,0,1:T(8,128)(2,1)} collective-permute-done((bf16[192,96,128]{2,0,1:T(8,128)(2,1)}, bf16[192,96,128]{2,0,1:T(8,128)(2,1)}, u32[]{:S(2)}, u32[]{:S(2)}) %collective-permute-start.2) | collective-permute-done | bytes 4718624 | tf_op jit(solution)/shard_map/ppermute | solution.py:110
  253.4 19.6 %fusion.15 = bf16[4,192,96,128]{3,1,2,0:T(8,128)(2,1)} fusion(bf16[192,96,128]{2,0,1:T(8,128)(2,1)} %collective-permute-done.2, bf16[192,96,128]{2,0,1:T(8,128)(2,1)} %collective-permute-done.1, bf16[192,96,128]{2,0,1:T(8,128)(2,1)} %collective-permute-done, bf16[192,96,128]{2,0,1:T(8,128)(2,1)S(1)} %copy.36, bf16[768,4,192,1]{0,2,1,3:T(8,128)(2,1)S(1)} %reshape.78), kind=kOutput, calls=%fused_computation.17 | convolution fusion | flops 14580449280 | bytes 38928384 | tf_op jit(solution)/shard_map/yzx,ydk->dkzx/dot_general | solution.py:147
  273.0 14.2 slice_bitcast_fusion.4
  287.2 2.0 collective-permute-start.5
  289.4 65.1 %collective-permute-done.8 = bf16[192,96,128]{2,0,1:T(8,128)(2,1)} collective-permute-done((bf16[192,96,128]{2,0,1:T(8,128)(2,1)}, bf16[192,96,128]{2,0,1:T(8,128)(2,1)}, u32[]{:S(2)}, u32[]{:S(2)}) %collective-permute-start.8) | collective-permute-done | bytes 4718624 | tf_op jit(solution)/shard_map/ppermute | solution.py:110
  355.0 1.5 copy.10
  356.4 6.5 copy.40
  362.9 5.3 copy.19
  368.2 87.8 %collective-permute-done.7 = bf16[192,96,128]{2,0,1:T(8,128)(2,1)} collective-permute-done((bf16[192,96,128]{2,0,1:T(8,128)(2,1)}, bf16[192,96,128]{2,0,1:T(8,128)(2,1)}, u32[]{:S(2)}, u32[]{:S(2)}) %collective-permute-start.7) | collective-permute-done | bytes 4718624 | tf_op jit(solution)/shard_map/ppermute | solution.py:110
  456.0 20.1 %fusion.14 = bf16[4,192,96,128]{3,1,2,0:T(8,128)(2,1)} fusion(bf16[192,96,128]{2,0,1:T(8,128)(2,1)} %collective-permute-done.8, bf16[192,96,128]{2,0,1:T(8,128)(2,1)} %collective-permute-done.7, bf16[192,96,128]{2,0,1:T(8,128)(2,1)} %collective-permute-done.6, bf16[192,96,128]{2,0,1:T(8,128)(2,1)} %copy.40, bf16[768,4,192,1]{0,2,1,3:T(8,128)(2,1)S(1)} %reshape.78), kind=kOutput, calls=%fused_computation.16 | convolution fusion | flops 14580449280 | bytes 38928384 | tf_op jit(solution)/shard_map/yzx,ydk->dkzx/dot_general | solution.py:147
  476.1 13.9 slice_bitcast_fusion
  490.0 66.7 %collective-permute-done.5 = bf16[192,96,128]{2,0,1:T(8,128)(2,1)} collective-permute-done((bf16[192,96,128]{2,0,1:T(8,128)(2,1)}, bf16[192,96,128]{2,0,1:T(8,128)(2,1)}, u32[]{:S(2)}, u32[]{:S(2)}) %collective-permute-start.5) | collective-permute-done | bytes 4718624 | tf_op jit(solution)/shard_map/ppermute | solution.py:110
  556.7 7.5 copy.22
  564.3 93.8 %collective-permute-done.4 = bf16[192,96,128]{2,0,1:T(8,128)(2,1)} collective-permute-done((bf16[192,96,128]{2,0,1:T(8,128)(2,1)}, bf16[192,96,128]{2,0,1:T(8,128)(2,1)}, u32[]{:S(2)}, u32[]{:S(2)}) %collective-permute-start.4) | collective-permute-done | bytes 4718624 | tf_op jit(solution)/shard_map/ppermute | solution.py:110
  658.0 7.5 copy.21
  665.5 7.5 copy.20
  673.0 148.5 %all-to-all-done = bf16[192,96,1024]{2,1,0:T(8,128)(2,1)} async-done(((bf16[192,96,1024]{2,1,0:T(8,128)(2,1)}), bf16[192,96,1024]{2,1,0:T(8,128)(2,1)}, u32[]{:S(2)}, u32[]{:S(2)}) %all-to-all-start) | async-done | bytes 37748768 | tf_op jit(solution)/shard_map/all_to_all | solution.py:130
  821.5 4.3 shard_map.75
  825.8 3.6 all-to-all-start.1
  829.4 38.7 %shard_map.74 = bf16[8,21,96,1024]{3,2,1,0:T(8,128)(2,1)} custom-call(bf16[768,768]{1,0:T(8,128)(2,1)} %bitcast.97, bf16[8,24,96,1024]{3,2,1,0:T(8,128)(2,1)} %bitcast.17.field_ref), custom_call_target="tpu_custom_call" | custom-call | flops 25367150592 | bytes 66060288 | tf_op jit(solution)/shard_map/pallas_call | solution.py:28
  869.2 7.1 all-to-all-start.3
  876.4 1.5 collective-permute-start.10
  878.3 7.6 copy.27
  885.9 6.0 shard_map.73
  891.9 7.5 copy.28
  899.5 81.9 %collective-permute-done.10 = bf16[192,96,128]{2,0,1:T(8,128)(2,1)} collective-permute-done((bf16[192,96,128]{2,0,1:T(8,128)(2,1)}, bf16[192,96,128]{2,0,1:T(8,128)(2,1)}, u32[]{:S(2)}, u32[]{:S(2)}) %collective-permute-start.10) | collective-permute-done | bytes 4718624 | tf_op jit(solution)/shard_map/ppermute | solution.py:110
  981.4 7.7 copy.29
  989.1 92.5 %collective-permute-done.11 = bf16[192,96,128]{2,0,1:T(8,128)(2,1)} collective-permute-done((bf16[192,96,128]{2,0,1:T(8,128)(2,1)}, bf16[192,96,128]{2,0,1:T(8,128)(2,1)}, u32[]{:S(2)}, u32[]{:S(2)}) %collective-permute-start.11) | collective-permute-done | bytes 4718624 | tf_op jit(solution)/shard_map/ppermute | solution.py:110
  1081.6 7.5 copy.30
  1089.2 5.1 shard_map.76.refs_8_
  1094.3 493.2 %all-to-all-done.3 = bf16[168,96,1024]{2,1,0:T(8,128)(2,1)} async-done(((bf16[168,96,1024]{2,1,0:T(8,128)(2,1)}), bf16[168,96,1024]{2,1,0:T(8,128)(2,1)}, u32[]{:S(2)}, u32[]{:S(2)}) %all-to-all-start.3) | async-done | bytes 33030176 | tf_op jit(solution)/shard_map/all_to_all | solution.py:173
  1587.6 4.6 all-to-all-start.2
  1592.2 2.3 copy-done
  1594.5 2.3 copy-done.2
  1596.9 2.3 copy-done.4
  1599.2 2.3 copy-done.6
  1601.5 2.3 copy-done.8
  1603.9 50.7 %shard_map.77.refs_8_ = bf16[8,24,96,1024]{3,2,1,0:T(8,128)(2,1)} custom-call(s32[1]{0:T(128)} %bitcast.row_ref, bf16[1024,1024]{1,0:T(8,128)(2,1)S(1)} %copy-done.9, bf16[8,24,96,1024]{3,2,1,0:T(8,128)(2,1)} %bitcast.75, bf16[8,21,96,1024]{3,2,1,0:T(8,128)(2,1)} %bitcast.27.z_ref, ...), custom_call_target="tpu_custom_call", output_to_operand_aliasing={{}: (12, {})} | custom-call | flops 33822867456 | bytes 132120576 | tf_op jit(solution)/shard_map/pallas_call | solution.py:90
  1654.6 7.8 all-to-all-done.2
  1662.4 2.3 copy-done.1
  1664.8 2.3 copy-done.3
  1667.1 2.3 copy-done.5
  1669.4 2.3 copy-done.7
  1671.8 7.6 shard_map.78
  (79 shorter events, 5.9 us)
Async XLA Ops:
  0.0 821.5 %all-to-all-start = ((bf16[192,96,1024]{2,1,0:T(8,128)(2,1)}), bf16[192,96,1024]{2,1,0:T(8,128)(2,1)}, u32[]{:S(2)}, u32[]{:S(2)}) async-start(bf16[192,96,1024]{2,1,0:T(8,128)(2,1)} %param.7), calls=%async_computation | async-start | bytes 75497472 | tf_op jit(solution)/shard_map/all_to_all | solution.py:130
  33.8 15.8 slice-start.12
  33.8 20.0 %slice-start.10 = ((s8[4718592]{0:T(1024)(128)(4,1)}), s8[4194304]{0:T(1024)(128)(4,1)S(1)}, s32[]{:S(2)}) async-start(s8[4718592]{0:T(1024)(128)(4,1)} %bitcast.89), calls=%async_computation.14 | async-start | bytes 8388608
  40.3 45.0 %collective-permute-start = (bf16[192,96,128]{2,0,1:T(8,128)(2,1)}, bf16[192,96,128]{2,0,1:T(8,128)(2,1)}, u32[]{:S(2)}, u32[]{:S(2)}) collective-permute-start(bf16[192,96,128]{2,0,1:T(8,128)(2,1)} %copy.37), channel_id=1, source_target_pairs={{0,8},{8,0},{16,24},{24,16},{1,9},{9,1},{17,25},{25,17},{2,10},{10... | collective-permute-start | bytes 14155784 | tf_op jit(solution)/shard_map/ppermute | solution.py:110
  40.8 8.9 slice-start.13
  40.8 13.0 slice-start.11
  47.2 105.5 %collective-permute-start.1 = (bf16[192,96,128]{2,0,1:T(8,128)(2,1)}, bf16[192,96,128]{2,0,1:T(8,128)(2,1)}, u32[]{:S(2)}, u32[]{:S(2)}) collective-permute-start(bf16[192,96,128]{2,0,1:T(8,128)(2,1)} %copy.38), channel_id=1, source_target_pairs={{0,16},{8,24},{16,0},{24,8},{1,17},{9,25},{17,1},{25,9},{2,18},{10... | collective-permute-start | bytes 14155784 | tf_op jit(solution)/shard_map/ppermute | solution.py:110
  49.7 9.7 slice-start.8
  53.7 199.7 %collective-permute-start.2 = (bf16[192,96,128]{2,0,1:T(8,128)(2,1)}, bf16[192,96,128]{2,0,1:T(8,128)(2,1)}, u32[]{:S(2)}, u32[]{:S(2)}) collective-permute-start(bf16[192,96,128]{2,0,1:T(8,128)(2,1)} %copy.39), channel_id=1, source_target_pairs={{0,24},{8,16},{16,8},{24,0},{1,25},{9,17},{17,9},{25,1},{2,26},{10... | collective-permute-start | bytes 14155784 | tf_op jit(solution)/shard_map/ppermute | solution.py:110
  53.8 5.5 slice-start.9
  57.7 296.7 %collective-permute-start.8 = (bf16[192,96,128]{2,0,1:T(8,128)(2,1)}, bf16[192,96,128]{2,0,1:T(8,128)(2,1)}, u32[]{:S(2)}, u32[]{:S(2)}) collective-permute-start(bf16[192,96,128]{2,0,1:T(8,128)(2,1)} %copy.43), channel_id=1, source_target_pairs={{0,24},{8,16},{16,8},{24,0},{1,25},{9,17},{17,9},{25,1},{2,26},{10... | collective-permute-start | bytes 14155784 | tf_op jit(solution)/shard_map/ppermute | solution.py:110
  59.4 4.2 copy-start.12
  59.4 4.2 copy-start.14
  59.4 4.2 copy-start.15
  63.3 304.8 %collective-permute-start.6 = (bf16[192,96,128]{2,0,1:T(8,128)(2,1)}, bf16[192,96,128]{2,0,1:T(8,128)(2,1)}, u32[]{:S(2)}, u32[]{:S(2)}) collective-permute-start(bf16[192,96,128]{2,0,1:T(8,128)(2,1)} %copy.41), channel_id=1, source_target_pairs={{0,8},{8,0},{16,24},{24,16},{1,9},{9,1},{17,25},{25,17},{2,10},{10... | collective-permute-start | bytes 14155784 | tf_op jit(solution)/shard_map/ppermute | solution.py:110
  85.3 370.7 %collective-permute-start.7 = (bf16[192,96,128]{2,0,1:T(8,128)(2,1)}, bf16[192,96,128]{2,0,1:T(8,128)(2,1)}, u32[]{:S(2)}, u32[]{:S(2)}) collective-permute-start(bf16[192,96,128]{2,0,1:T(8,128)(2,1)} %copy.42), channel_id=1, source_target_pairs={{0,16},{8,24},{16,0},{24,8},{1,17},{9,25},{17,1},{25,9},{2,18},{10... | collective-permute-start | bytes 14155784 | tf_op jit(solution)/shard_map/ppermute | solution.py:110
  273.0 82.0 %copy-start.13 = (bf16[768,768]{1,0:T(8,128)(2,1)S(1)}, bf16[768,768]{1,0:T(8,128)(2,1)}, u32[]{:S(2)}) copy-start(bf16[768,768]{1,0:T(8,128)(2,1)} %param.13) | copy-start | bytes 3538948
  287.2 269.5 %collective-permute-start.5 = (bf16[192,96,128]{2,0,1:T(8,128)(2,1)}, bf16[192,96,128]{2,0,1:T(8,128)(2,1)}, u32[]{:S(2)}, u32[]{:S(2)}) collective-permute-start(bf16[192,96,128]{2,0,1:T(8,128)(2,1)} %get-tuple-element.43), channel_id=1, source_target_pairs={{0,24},{8,16},{16,8},{24,0},{1,25},{9,17},{17,9},{25,1},{2,26},{10... | collective-permute-start | bytes 14155784 | tf_op jit(solution)/shard_map/ppermute | solution.py:110
  289.3 368.8 %collective-permute-start.4 = (bf16[192,96,128]{2,0,1:T(8,128)(2,1)}, bf16[192,96,128]{2,0,1:T(8,128)(2,1)}, u32[]{:S(2)}, u32[]{:S(2)}) collective-permute-start(bf16[192,96,128]{2,0,1:T(8,128)(2,1)} %get-tuple-element.44), channel_id=1, source_target_pairs={{0,16},{8,24},{16,0},{24,8},{1,17},{9,25},{17,1},{25,9},{2,18},{10... | collective-permute-start | bytes 14155784 | tf_op jit(solution)/shard_map/ppermute | solution.py:110
  354.5 311.0 %collective-permute-start.3 = (bf16[192,96,128]{2,0,1:T(8,128)(2,1)}, bf16[192,96,128]{2,0,1:T(8,128)(2,1)}, u32[]{:S(2)}, u32[]{:S(2)}) collective-permute-start(bf16[192,96,128]{2,0,1:T(8,128)(2,1)} %get-tuple-element.45), channel_id=1, source_target_pairs={{0,8},{8,0},{16,24},{24,16},{1,9},{9,1},{17,25},{25,17},{2,10},{10... | collective-permute-start | bytes 14155784 | tf_op jit(solution)/shard_map/ppermute | solution.py:110
  355.0 7.9 slice-start.14
  356.4 6.5 slice-start.15
  825.8 42.3 %all-to-all-start.1 = ((bf16[8,96,1024]{2,1,0:T(8,128)(2,1)}), bf16[8,96,1024]{2,1,0:T(8,128)(2,1)S(1)}, u32[]{:S(2)}, u32[]{:S(2)}) async-start(bf16[8,96,1024]{2,1,0:T(8,128)(2,1)} %bitcast.99), calls=%async_computation.1 | async-start | bytes 3145728 | tf_op jit(solution)/shard_map/all_to_all | solution.py:173
  868.1 1.1 copy-start.10
  869.2 718.3 %all-to-all-start.3 = ((bf16[168,96,1024]{2,1,0:T(8,128)(2,1)}), bf16[168,96,1024]{2,1,0:T(8,128)(2,1)}, u32[]{:S(2)}, u32[]{:S(2)}) async-start(bf16[168,96,1024]{2,1,0:T(8,128)(2,1)} %bitcast.86), calls=%async_computation.3 | async-start | bytes 66060288 | tf_op jit(solution)/shard_map/all_to_all | solution.py:173
  876.3 15.6 collective-permute-start.9
  876.4 105.0 %collective-permute-start.10 = (bf16[192,96,128]{2,0,1:T(8,128)(2,1)}, bf16[192,96,128]{2,0,1:T(8,128)(2,1)}, u32[]{:S(2)}, u32[]{:S(2)}) collective-permute-start(bf16[192,96,128]{2,0,1:T(8,128)(2,1)} %get-tuple-element.26), channel_id=1, source_target_pairs={{0,16},{8,24},{16,0},{24,8},{1,17},{9,25},{17,1},{25,9},{2,18},{10... | collective-permute-start | bytes 14155784 | tf_op jit(solution)/shard_map/ppermute | solution.py:110
  877.9 203.7 %collective-permute-start.11 = (bf16[192,96,128]{2,0,1:T(8,128)(2,1)}, bf16[192,96,128]{2,0,1:T(8,128)(2,1)}, u32[]{:S(2)}, u32[]{:S(2)}) collective-permute-start(bf16[192,96,128]{2,0,1:T(8,128)(2,1)} %get-tuple-element.27), channel_id=1, source_target_pairs={{0,24},{8,16},{16,8},{24,0},{1,25},{9,17},{17,9},{25,1},{2,26},{10... | collective-permute-start | bytes 14155784 | tf_op jit(solution)/shard_map/ppermute | solution.py:110
  878.3 210.9 %slice-start.6 = ((s8[4718592]{0:T(1024)(128)(4,1)}), s8[4194304]{0:T(1024)(128)(4,1)S(1)}, s32[]{:S(2)}) async-start(s8[4718592]{0:T(1024)(128)(4,1)} %bitcast.65), calls=%async_computation.10 | async-start | bytes 8388608
  885.9 203.2 %slice-start.7 = ((s8[4718592]{0:T(1024)(128)(4,1)}), s8[524288]{0:T(1024)(128)(4,1)S(1)}, s32[]{:S(2)}) async-start(s8[4718592]{0:T(1024)(128)(4,1)} %bitcast.65), calls=%async_computation.11 | async-start | bytes 1048576
  981.4 107.8 %slice-start = ((s8[4718592]{0:T(1024)(128)(4,1)}), s8[4194304]{0:T(1024)(128)(4,1)S(1)}, s32[]{:S(2)}) async-start(s8[4718592]{0:T(1024)(128)(4,1)} %bitcast.50), calls=%async_computation.4 | async-start | bytes 8388608
  981.4 107.8 %slice-start.2 = ((s8[4718592]{0:T(1024)(128)(4,1)}), s8[4194304]{0:T(1024)(128)(4,1)S(1)}, s32[]{:S(2)}) async-start(s8[4718592]{0:T(1024)(128)(4,1)} %bitcast.55), calls=%async_computation.6 | async-start | bytes 8388608
  981.4 107.8 %slice-start.4 = ((s8[4718592]{0:T(1024)(128)(4,1)}), s8[4194304]{0:T(1024)(128)(4,1)S(1)}, s32[]{:S(2)}) async-start(s8[4718592]{0:T(1024)(128)(4,1)} %bitcast.60), calls=%async_computation.8 | async-start | bytes 8388608
  989.1 100.1 %slice-start.1 = ((s8[4718592]{0:T(1024)(128)(4,1)}), s8[524288]{0:T(1024)(128)(4,1)S(1)}, s32[]{:S(2)}) async-start(s8[4718592]{0:T(1024)(128)(4,1)} %bitcast.50), calls=%async_computation.5 | async-start | bytes 1048576
  989.1 100.1 %slice-start.3 = ((s8[4718592]{0:T(1024)(128)(4,1)}), s8[524288]{0:T(1024)(128)(4,1)S(1)}, s32[]{:S(2)}) async-start(s8[4718592]{0:T(1024)(128)(4,1)} %bitcast.55), calls=%async_computation.7 | async-start | bytes 1048576
  989.1 100.1 %slice-start.5 = ((s8[4718592]{0:T(1024)(128)(4,1)}), s8[524288]{0:T(1024)(128)(4,1)S(1)}, s32[]{:S(2)}) async-start(s8[4718592]{0:T(1024)(128)(4,1)} %bitcast.60), calls=%async_computation.9 | async-start | bytes 1048576
  989.1 100.1 %copy-start.9 = (bf16[1024,1024]{1,0:T(8,128)(2,1)S(1)}, bf16[1024,1024]{1,0:T(8,128)(2,1)}, u32[]{:S(2)}) copy-start(bf16[1024,1024]{1,0:T(8,128)(2,1)} %operator_ref.5) | copy-start | bytes 6291460
  989.1 100.1 %copy-start.11 = (bf16[8,96,1024]{2,1,0:T(8,128)(2,1)S(1)}, bf16[8,96,1024]{2,1,0:T(8,128)(2,1)}, u32[]{:S(2)}) copy-start(bf16[8,96,1024]{2,1,0:T(8,128)(2,1)} %copy-done.10) | copy-start | bytes 4718596
  1587.6 74.9 %all-to-all-start.2 = ((bf16[16,96,1024]{2,1,0:T(8,128)(2,1)}), bf16[16,96,1024]{2,1,0:T(8,128)(2,1)}, u32[]{:S(2)}, u32[]{:S(2)}) async-start(bf16[16,96,1024]{2,1,0:T(8,128)(2,1)} %bitcast.95), calls=%async_computation.2 | async-start | bytes 6291456 | tf_op jit(solution)/shard_map/all_to_all | solution.py:173
  1592.2 2.3 copy-start
  1594.5 2.3 copy-start.2
  1596.9 2.3 copy-start.4
  1599.2 2.3 copy-start.6
  1601.5 2.3 copy-start.8
  1662.4 2.3 copy-start.1
  1664.8 2.3 copy-start.3
  1667.1 2.3 copy-start.5
  1669.4 2.3 copy-start.7

commit v3 on v2

--- a/solution.py
+++ b/solution.py
@@ -8,7 +8,7 @@
 from jax.experimental.pallas import tpu as pltpu
 from jax.sharding import PartitionSpec as P
 
-VMEM_BYTES = 56 * 1024 * 1024
+VMEM_BYTES = 62 * 1024 * 1024
 
 
 def z_kernel(operator_ref, field_ref, out_ref):
@@ -25,14 +25,16 @@
 def z_apply(operator, field, first, count):
     parts, rows, depth, width = field.shape
     points = parts * depth
+    step = math.gcd(math.gcd(first, count), 2)
+    skip = first // step
     return pl.pallas_call(
         z_kernel,
-        grid=(count,),
+        grid=(count // step,),
         in_specs=[
             pl.BlockSpec((points, points), lambda i: (0, 0)),
-            pl.BlockSpec((parts, 1, depth, width), lambda i: (0, i + first, 0, 0)),
+            pl.BlockSpec((parts, step, depth, width), lambda i: (0, i + skip, 0, 0)),
         ],
-        out_specs=pl.BlockSpec((parts, 1, depth, width), lambda i: (0, i, 0, 0)),
+        out_specs=pl.BlockSpec((parts, step, depth, width), lambda i: (0, i, 0, 0)),
         out_shape=jax.ShapeDtypeStruct((parts, count, depth, width), jnp.bfloat16),
         compiler_params=pltpu.CompilerParams(vmem_limit_bytes=VMEM_BYTES),
         cost_estimate=pl.CostEstimate(
@@ -43,8 +45,47 @@
     )(operator, field)
 
 
-def total_kernel(slabs, row_ref, operator_ref, field_ref, z_ref, *refs):
-    y_refs, out_ref = refs[: 2 * slabs], refs[-1]
+def z_pieces_kernel(operator_ref, field_ref, *out_refs):
+    parts, _, depth, width = field_ref.shape
+    planes = field_ref[:, 0]
+    if depth % 16:
+        planes = planes.astype(jnp.float32)
+    planes = planes.reshape(parts * depth, width).astype(jnp.bfloat16)
+    product = jnp.dot(operator_ref[...], planes, preferred_element_type=jnp.float32)
+    for part, out_ref in enumerate(out_refs):
+        out_ref[0] = product[part * depth : (part + 1) * depth].astype(jnp.bfloat16)
+
+
+def z_pieces(operator, field, first, count):
+    parts, _, depth, width = field.shape
+    points = parts * depth
+    return pl.pallas_call(
+        z_pieces_kernel,
+        grid=(count,),
+        in_specs=[
+            pl.BlockSpec((points, points), lambda i: (0, 0)),
+            pl.BlockSpec((parts, 1, depth, width), lambda i: (0, i + first, 0, 0)),
+        ],
+        out_specs=[pl.BlockSpec((1, depth, width), lambda i: (i, 0, 0))] * parts,
+        out_shape=[jax.ShapeDtypeStruct((count, depth, width), jnp.bfloat16)] * parts,
+        compiler_params=pltpu.CompilerParams(vmem_limit_bytes=VMEM_BYTES),
+        cost_estimate=pl.CostEstimate(
+            flops=2 * points * points * count * width,
+            bytes_accessed=4 * points * count * width,
+            transcendentals=0,
+        ),
+    )(operator, field)
+
+
+def total_kernel(slabs, pieces, place_ref, operator_ref, field_ref, *refs):
+    if pieces > 1:
+        z_ref = refs[-1]
+        for distance in range(pieces):
+            z_ref[place_ref[1] ^ distance] = refs[distance][...]
+        out_ref = refs[-2]
+    else:
+        z_ref, out_ref = refs[0], refs[-1]
+    y_refs = refs[pieces : pieces + 2 * slabs]
     parts, rows, depth, width = out_ref.shape
     slab = width // slabs
     share = slab // 2
@@ -66,44 +107,52 @@
                 out_ref[:, :, :, here] = (x_term + y_term + z_term).astype(jnp.bfloat16)
 
     for me in range(slabs):
-        pl.when(row_ref[0] == me)(functools.partial(add_all, me))
-
-
-def total_into(so_far, first, together, row, operator, field, z_term, y_terms):
-    parts, count, depth, width = z_term.shape
+        pl.when(place_ref[0] == me)(functools.partial(add_all, me))
+
+
+def total_into(so_far, first, together, place, operator, field, z_terms, y_terms):
+    parts, _, depth, width = field.shape
     share = y_terms[0].shape[3]
     here = pl.BlockSpec((together, 1, depth, width), lambda p, i, r: (p, i + first, 0, 0))
-    in_specs = [
-        pl.BlockSpec((width, width), lambda p, i, r: (0, 0)),
-        here,
-        pl.BlockSpec((together, 1, depth, width), lambda p, i, r: (p, i, 0, 0)),
-    ] + [
+    scratch = []
+    if len(z_terms) == 1:
+        count = z_terms[0].shape[1]
+        z_spec = pl.BlockSpec((together, 1, depth, width), lambda p, i, r: (p, i, 0, 0))
+    else:
+        count, together = z_terms[0].shape[0], parts
+        here = pl.BlockSpec((parts, 1, depth, width), lambda p, i, r: (p, i + first, 0, 0))
+        z_spec = pl.BlockSpec((1, depth, width), lambda p, i, r: (i, 0, 0))
+        scratch = [pltpu.VMEM((parts, 1, depth, width), jnp.bfloat16)]
+    in_specs = [pl.BlockSpec((width, width), lambda p, i, r: (0, 0)), here]
+    in_specs += [z_spec] * len(z_terms)
+    in_specs += [
         pl.BlockSpec((together, 1, depth, share), lambda p, i, r: (p, i + first, 0, 0))
         for _ in y_terms
     ]
-    operands = [operator, field, z_term, *y_terms]
+    operands = [operator, field, *z_terms, *y_terms]
     aliases = {}
     if so_far is not None:
         in_specs.append(pl.BlockSpec(memory_space=pl.ANY))
         operands.append(so_far)
         aliases = {len(operands): 0}
     return pl.pallas_call(
-        functools.partial(total_kernel, len(y_terms) // 2),
+        functools.partial(total_kernel, len(y_terms) // 2, len(z_terms)),
         grid_spec=pltpu.PrefetchScalarGridSpec(
             num_scalar_prefetch=1,
             grid=(parts // together, count),
             in_specs=in_specs,
             out_specs=here,
+            scratch_shapes=scratch,
         ),
         out_shape=jax.ShapeDtypeStruct(field.shape, jnp.bfloat16),
         input_output_aliases=aliases,
-        compiler_params=pltpu.CompilerParams(vmem_limit_bytes=VMEM_BYTES // 2),
+        compiler_params=pltpu.CompilerParams(vmem_limit_bytes=VMEM_BYTES),
         cost_estimate=pl.CostEstimate(
             flops=2 * width * width * parts * count * depth,
             bytes_accessed=8 * width * parts * count * depth,
             transcendentals=0,
         ),
-    )(row, *operands)
+    )(place, *operands)
 
 
 def swap(value, axis, size, distance):
@@ -111,10 +160,8 @@
 
 
 def chunk_sizes(share):
-    if share < 3:
-        return [share]
-    last = 2 if share >= 12 else 1
-    return [1, share - 1 - last, last]
+    few = 2 if share >= 12 else 1
+    return few, share - 2 * few, few
 
 
 def per_device(rows, cols, scalar_field, x_operator, y_second, y_first, y_stretch, y_curve, z_operator):
@@ -159,38 +206,42 @@
     planes, y_first_half, y_second_half = lax.optimization_barrier(
         (planes, y_first_half, y_second_half)
     )
-    y_second_half = y_return(y_second_half)
+    y_terms = y_first_half + y_return(y_second_half)
 
     planes = planes.reshape(cols, share, nz, nx)
     field = scalar_field.reshape(cols, share, nz, nx)
-    where = me.reshape(1).astype(jnp.int32)
+    col = lax.axis_index("col")
+    place = jnp.stack([me, col]).astype(jnp.int32)
+    z_blocks = z_transposed.reshape(cols, nz, cols * nz)
+    z_by_distance = jnp.concatenate([z_blocks[col ^ d] for d in range(cols)], axis=0)
     sizes = chunk_sizes(share)
     starts = [sum(sizes[:c]) for c in range(len(sizes))]
-    last = len(sizes) - 1
+
+    def z_swap(pieces):
+        return [pieces[d] if d == 0 else swap(pieces[d], "col", cols, d) for d in range(cols)]
 
     def z_return(product):
         flat = product.reshape(-1, nz, nx)
         return lax.all_to_all(flat, "col", 0, 0, tiled=True).reshape(product.shape)
 
-    def add_chunk(result, c):
-        together = math.gcd(cols, 4 if c == last else 8)
-        y_terms = y_first_half + y_second_half
+    def add_chunk(result, c, together, z_terms):
         return total_into(
-            result, starts[c], together, where, x_operator, field, z_back[c], y_terms
+            result, starts[c], together, place, x_operator, field, z_terms, y_terms
         )
 
-    z_back, result = [], None
-    for c in range(len(sizes)):
-        product = z_apply(z_transposed, planes, starts[c], sizes[c])
-        if c == last and last > 0:
-            for earlier in range(last - 1):
-                result = add_chunk(result, earlier)
-            product, result = lax.optimization_barrier((product, result))
-        elif c > 0:
-            product, z_back[c - 1] = lax.optimization_barrier((product, z_back[c - 1]))
-        z_back.append(z_return(product))
-    for c in range(max(last - 1, 0), len(sizes)):
-        result = add_chunk(result, c)
+    far = cols // 2
+    z_first = z_swap(z_pieces(z_by_distance, planes, starts[0], sizes[0]))
+    bulk = z_apply(z_transposed, planes, starts[1], sizes[1])
+    bulk, planes, z_first[far:] = lax.optimization_barrier((bulk, planes, z_first[far:]))
+    z_bulk = z_return(bulk)
+
+    product = z_apply(z_transposed, planes, starts[2], sizes[2])
+    result = add_chunk(None, 0, cols, z_first)
+    product, result = lax.optimization_barrier((product, result))
+    z_last = z_return(product)
+
+    result = add_chunk(result, 1, cols, [z_bulk])
+    result = add_chunk(result, 2, math.gcd(cols, 4), [z_last])
     return result.reshape(ny, nz, nx)
 
 

time: 1680 us -> 1670 us (level)
  starting transfers between devices: 32.6 us -> 64.8 us
  waiting for transfers between devices: 1300 us -> 1270 us
  local copies, waits for them, and re-layouts: 189 us -> 168 us
    all_to_all x3 -> x2, waiting for transfers between devices: 501 us -> 164 us  [z_return(): return lax.all_to_all(flat, 'col', 0, 0, tiled=True).reshape(product.shape)]
    ppermute x12 -> x19, waiting for transfers between devices: 648 us -> 959 us  [swap(): return lax.ppermute(value, axis, [(i, i ^ distance) for i in range(size)])]
    unnamed x77 -> x64, local copies, waits for them, and re-layouts: 72.4 us -> 52.1 us
    ppermute x12 -> x19, starting transfers between devices: 9.83 us -> 29.4 us  [swap(): return lax.ppermute(value, axis, [(i, i ^ distance) for i in range(size)])]
  transfers between devices with their start and end apart: 16 -> 22, of which waited for: 11 -> 17; matrix products, arithmetic and copies ran while one was open for 13% -> 13% of each run, Pallas kernels for 6% -> 6%
where the time goes in v3:
time: 1670 us
  waiting for transfers between devices  1270 us (76%)
  local copies, waits for them, and re-layouts  168 us (10%)
  Pallas kernels  116 us (7%)
  starting transfers between devices  64.8 us (4%)
  matrix products  41.2 us (2%)
    ppermute x19, waiting for transfers between devices, swap(): return lax.ppermute(value, axis, [(i, i ^ distance) for i in range(size)])  959 us
    all_to_all x2, waiting for transfers between devices, z_return(): return lax.all_to_all(flat, 'col', 0, 0, tiled=True).reshape(product.shape)  164 us
    all_to_all x1, waiting for transfers between devices, per_device(): planes = lax.all_to_all(scalar_field, 'col', 0, 0, tiled=True)  148 us
    pallas_call x3, Pallas kernels, total_into(): pl.pallas_call(functools.partial(total_kernel, len(y_terms) // 2, len(z_t...  71.4 us
    unnamed x64, local copies, waits for them, and re-layouts  52.1 us
    ppermute x6, local copies, waits for them, and re-layouts, swap(): return lax.ppermute(value, axis, [(i, i ^ distance) for i in range(size)])  45.4 us
    dot_general x2, matrix products, y_multiply(): jnp.einsum('yzx,ydk->dkzx', pencil, by_distance, preferred_element_type=j...  41.2 us
    pallas_call x2, Pallas kernels, z_apply(): pl.pallas_call(z_kernel, grid=(count // step,), in_specs=[pl.BlockSpec((p...  38.6 us
  transfers between devices with their start and end apart: 22, of which 17 were waited for; matrix products, arithmetic and copies ran while one was open for 13% of the time, Pallas kernels for 6%

profile of v3, /device:TPU:0, one launch (start us, length us, event | category | flops | bytes accessed | tf_op | source)
XLA Modules:
  0.0 1671.2 jit_solution(2676927256627460918)
XLA Ops:
  0.0 7.5 all-to-all-start
  7.6 26.2 %constant_dynamic-slice_fusion.3 = (bf16[192,96,128]{2,1,0:T(8,128)(2,1)}, bf16[192,96,128]{2,1,0:T(8,128)(2,1)}, bf16[192,96,128]{2,1,0:T(8,128)(2,1)}, bf16[19...) fusion(bf16[192,96,1024]{2,1,0:T(8,128)(2,1)} %param.7, ...), kind=kLoop, calls=%fused_computation.41 | loop fusion | bytes 75497504 | tf_op jit(solution)/shard_map/dynamic_slice | solution.py:189
  33.8 6.5 copy.37
  40.7 6.4 copy.38
  47.2 2.5 collective-permute-start.1
  49.7 4.1 copy.39
  53.9 3.9 copy.43
  57.8 1.6 collective-permute-start.8
  59.5 3.9 copy.41
  63.6 1.7 add_convert_fusion
  65.3 1.4 reshape.54
  67.3 1.9 copy.32
  69.2 1.7 copy.34
  71.0 1.7 copy.33
  72.7 1.7 copy.35
  74.4 4.1 pad_maximum_fusion
  79.1 1.6 copy.10
  80.7 2.4 pad_maximum_fusion.1
  83.1 4.0 reshape.70
  87.1 6.4 copy.40
  93.5 6.4 copy.42
  99.9 3.9 copy.36
  104.3 48.4 %collective-permute-done.1 = bf16[192,96,128]{2,0,1:T(8,128)(2,1)} collective-permute-done((bf16[192,96,128]{2,0,1:T(8,128)(2,1)}, bf16[192,96,128]{2,0,1:T(8,128)(2,1)}, u32[]{:S(2)}, u32[]{:S(2)}) %collective-permute-start.1) | collective-permute-done | bytes 4718624 | tf_op jit(solution)/shard_map/ppermute | solution.py:159
  152.6 100.8 %collective-permute-done.2 = bf16[192,96,128]{2,0,1:T(8,128)(2,1)} collective-permute-done((bf16[192,96,128]{2,0,1:T(8,128)(2,1)}, bf16[192,96,128]{2,0,1:T(8,128)(2,1)}, u32[]{:S(2)}, u32[]{:S(2)}) %collective-permute-start.2) | collective-permute-done | bytes 4718624 | tf_op jit(solution)/shard_map/ppermute | solution.py:159
  253.4 20.9 %fusion.15 = bf16[4,192,96,128]{3,1,2,0:T(8,128)(2,1)} fusion(bf16[192,96,128]{2,0,1:T(8,128)(2,1)} %collective-permute-done.2, bf16[192,96,128]{2,0,1:T(8,128)(2,1)} %collective-permute-done.1, bf16[192,96,128]{2,0,1:T(8,128)(2,1)} %collective-permute-done, bf16[192,96,128]{2,0,1:T(8,128)(2,1)} %copy.36, bf16[768,4,192,1]{0,2,1,3:T(8,128)(2,1)} %reshape.70), kind=kOutput, calls=%fused_computation.17 | convolution fusion | flops 14580449280 | bytes 38928384 | tf_op jit(solution)/shard_map/yzx,ydk->dkzx/dot_general | solution.py:194
  274.3 11.0 slice_bitcast_fusion.4
  285.3 2.0 collective-permute-start.5
  287.4 67.1 %collective-permute-done.8 = bf16[192,96,128]{2,0,1:T(8,128)(2,1)} collective-permute-done((bf16[192,96,128]{2,0,1:T(8,128)(2,1)}, bf16[192,96,128]{2,0,1:T(8,128)(2,1)}, u32[]{:S(2)}, u32[]{:S(2)}) %collective-permute-start.8) | collective-permute-done | bytes 4718624 | tf_op jit(solution)/shard_map/ppermute | solution.py:159
  355.1 5.2 copy.19
  360.3 95.7 %collective-permute-done.7 = bf16[192,96,128]{2,0,1:T(8,128)(2,1)} collective-permute-done((bf16[192,96,128]{2,0,1:T(8,128)(2,1)}, bf16[192,96,128]{2,0,1:T(8,128)(2,1)}, u32[]{:S(2)}, u32[]{:S(2)}) %collective-permute-start.7) | collective-permute-done | bytes 4718624 | tf_op jit(solution)/shard_map/ppermute | solution.py:159
  456.0 20.3 %fusion.14 = bf16[4,192,96,128]{3,1,2,0:T(8,128)(2,1)} fusion(bf16[192,96,128]{2,0,1:T(8,128)(2,1)} %collective-permute-done.8, bf16[192,96,128]{2,0,1:T(8,128)(2,1)} %collective-permute-done.7, bf16[192,96,128]{2,0,1:T(8,128)(2,1)} %collective-permute-done.6, bf16[192,96,128]{2,0,1:T(8,128)(2,1)} %copy.40, bf16[768,4,192,1]{0,2,1,3:T(8,128)(2,1)S(1)} %copy-done.3), kind=kOutput, calls=%fused_computation.16 | convolution fusion | flops 14580449280 | bytes 38928384 | tf_op jit(solution)/shard_map/yzx,ydk->dkzx/dot_general | solution.py:194
  476.3 13.9 slice_bitcast_fusion
  490.2 66.6 %collective-permute-done.5 = bf16[192,96,128]{2,0,1:T(8,128)(2,1)} collective-permute-done((bf16[192,96,128]{2,0,1:T(8,128)(2,1)}, bf16[192,96,128]{2,0,1:T(8,128)(2,1)}, u32[]{:S(2)}, u32[]{:S(2)}) %collective-permute-start.5) | collective-permute-done | bytes 4718624 | tf_op jit(solution)/shard_map/ppermute | solution.py:159
  556.7 7.5 copy.22
  564.3 93.8 %collective-permute-done.4 = bf16[192,96,128]{2,0,1:T(8,128)(2,1)} collective-permute-done((bf16[192,96,128]{2,0,1:T(8,128)(2,1)}, bf16[192,96,128]{2,0,1:T(8,128)(2,1)}, u32[]{:S(2)}, u32[]{:S(2)}) %collective-permute-start.4) | collective-permute-done | bytes 4718624 | tf_op jit(solution)/shard_map/ppermute | solution.py:159
  658.0 7.6 copy.21
  665.6 7.5 copy.20
  673.1 148.4 %all-to-all-done = bf16[192,96,1024]{2,1,0:T(8,128)(2,1)} async-done(((bf16[192,96,1024]{2,1,0:T(8,128)(2,1)}), bf16[192,96,1024]{2,1,0:T(8,128)(2,1)}, u32[]{:S(2)}, u32[]{:S(2)}) %all-to-all-start) | async-done | bytes 37748768 | tf_op jit(solution)/shard_map/all_to_all | solution.py:177
  821.5 5.5 shard_map.74
  827.1 3.7 collective-permute-start.10
  832.1 2.6 collective-permute-start.12
  834.7 32.1 %shard_map.73 = bf16[8,20,96,1024]{3,2,1,0:T(8,128)(2,1)} custom-call(bf16[768,768]{1,0:T(8,128)(2,1)} %bitcast.112, bf16[8,24,96,1024]{3,2,1,0:T(8,128)(2,1)} %bitcast.18.field_ref), custom_call_target="tpu_custom_call" | custom-call | flops 24159191040 | bytes 62914560 | tf_op jit(solution)/shard_map/pallas_call | solution.py:30
  866.8 5.9 collective-permute-done.9.refs_4_
  872.7 8.2 collective-permute-done.10.refs_5_
  882.0 19.2 %all-to-all-start.2 = ((bf16[160,96,1024]{2,1,0:T(8,128)(2,1)}), bf16[160,96,1024]{2,1,0:T(8,128)(2,1)}, u32[]{:S(2)}, u32[]{:S(2)}) async-start(bf16[160,96,1024]{2,1,0:T(8,128)(2,1)} %bitcast.94), calls=%async_computation.2 | async-start | bytes 62914560 | tf_op jit(solution)/shard_map/all_to_all | solution.py:225
  903.1 2.0 collective-permute-start.13
  905.1 4.2 collective-permute-start.14
  909.5 5.7 collective-permute-start.15
  915.8 7.5 copy.27
  923.3 6.6 shard_map.75
  929.9 7.5 copy.28
  937.4 68.9 %collective-permute-done.17 = bf16[192,96,128]{2,0,1:T(8,128)(2,1)} collective-permute-done((bf16[192,96,128]{2,0,1:T(8,128)(2,1)}, bf16[192,96,128]{2,0,1:T(8,128)(2,1)}, u32[]{:S(2)}, u32[]{:S(2)}) %collective-permute-start.17) | collective-permute-done | bytes 4718624 | tf_op jit(solution)/shard_map/ppermute | solution.py:159
  1006.2 7.5 copy.29
  1013.7 92.7 %collective-permute-done.18 = bf16[192,96,128]{2,0,1:T(8,128)(2,1)} collective-permute-done((bf16[192,96,128]{2,0,1:T(8,128)(2,1)}, bf16[192,96,128]{2,0,1:T(8,128)(2,1)}, u32[]{:S(2)}, u32[]{:S(2)}) %collective-permute-start.18) | collective-permute-done | bytes 4718624 | tf_op jit(solution)/shard_map/ppermute | solution.py:159
  1106.5 7.9 copy.30
  1114.3 48.0 %collective-permute-done.13.refs_1_ = bf16[2,96,1024]{2,1,0:T(8,128)(2,1)S(1)} collective-permute-done((bf16[2,96,1024]{2,1,0:T(8,128)(2,1)}, bf16[2,96,1024]{2,1,0:T(8,128)(2,1)S(1)}, u32[]{:S(2)}, u32[]{:S(2)}) %collective-permute-start.13) | collective-permute-done | bytes 393248 | tf_op jit(solution)/shard_map/ppermute | solution.py:159
  1162.4 256.2 %collective-permute-done.14.refs_2_ = bf16[2,96,1024]{2,1,0:T(8,128)(2,1)S(1)} collective-permute-done((bf16[2,96,1024]{2,1,0:T(8,128)(2,1)}, bf16[2,96,1024]{2,1,0:T(8,128)(2,1)S(1)}, u32[]{:S(2)}, u32[]{:S(2)}) %collective-permute-start.14) | collective-permute-done | bytes 393248 | tf_op jit(solution)/shard_map/ppermute | solution.py:159
  1418.5 7.1 collective-permute-done.15.refs_3_
  1426.3 9.0 shard_map.76.refs_9_
  1435.3 146.6 %all-to-all-done.2 = bf16[160,96,1024]{2,1,0:T(8,128)(2,1)} async-done(((bf16[160,96,1024]{2,1,0:T(8,128)(2,1)}), bf16[160,96,1024]{2,1,0:T(8,128)(2,1)}, u32[]{:S(2)}, u32[]{:S(2)}) %all-to-all-start.2) | async-done | bytes 31457312 | tf_op jit(solution)/shard_map/all_to_all | solution.py:225
  1581.9 8.7 all-to-all-start.1
  1590.7 53.0 %shard_map.77.refs_9_ = bf16[8,24,96,1024]{3,2,1,0:T(8,128)(2,1)} custom-call(s32[2]{0:T(128)} %pad_add_fusion.place_ref, bf16[1024,1024]{1,0:T(8,128)(2,1)} %operator_ref.5, bf16[8,24,96,1024]{3,2,1,0:T(8,128)(2,1)} %bitcast.68, bf16[8,20,96,1024]{3,2,1,0:T(8,128)(2,1)} %bitcast.36.refs_0_, ...), custom_call_target="tpu_custom_call", output_to_operand_aliasing={{}: (12, {})} | custom-call | flops 32212254720 | bytes 125829120 | tf_op jit(solution)/shard_map/pallas_call | solution.py:138
  1643.7 17.9 %all-to-all-done.1 = bf16[16,96,1024]{2,1,0:T(8,128)(2,1)} async-done(((bf16[16,96,1024]{2,1,0:T(8,128)(2,1)}), bf16[16,96,1024]{2,1,0:T(8,128)(2,1)}, u32[]{:S(2)}, u32[]{:S(2)}) %all-to-all-start.1) | async-done | bytes 3145760 | tf_op jit(solution)/shard_map/all_to_all | solution.py:225
  1661.6 9.4 shard_map.78
  (76 shorter events, 8.9 us)
Async XLA Ops:
  0.0 821.5 %all-to-all-start = ((bf16[192,96,1024]{2,1,0:T(8,128)(2,1)}), bf16[192,96,1024]{2,1,0:T(8,128)(2,1)}, u32[]{:S(2)}, u32[]{:S(2)}) async-start(bf16[192,96,1024]{2,1,0:T(8,128)(2,1)} %param.7), calls=%async_computation | async-start | bytes 75497472 | tf_op jit(solution)/shard_map/all_to_all | solution.py:177
  33.8 15.9 slice-start.6
  33.8 20.1 %slice-start.4 = ((s8[4718592]{0:T(1024)(128)(4,1)}), s8[4194304]{0:T(1024)(128)(4,1)S(1)}, s32[]{:S(2)}) async-start(s8[4718592]{0:T(1024)(128)(4,1)} %bitcast.99), calls=%async_computation.7 | async-start | bytes 8388608
  40.3 63.6 %collective-permute-start = (bf16[192,96,128]{2,0,1:T(8,128)(2,1)}, bf16[192,96,128]{2,0,1:T(8,128)(2,1)}, u32[]{:S(2)}, u32[]{:S(2)}) collective-permute-start(bf16[192,96,128]{2,0,1:T(8,128)(2,1)} %copy.37), channel_id=1, source_target_pairs={{0,8},{8,0},{16,24},{24,16},{1,9},{9,1},{17,25},{25,17},{2,10},{10... | collective-permute-start | bytes 14155784 | tf_op jit(solution)/shard_map/ppermute | solution.py:159
  40.7 8.9 slice-start.7
  40.7 13.1 slice-start.5
  47.2 105.5 %collective-permute-start.1 = (bf16[192,96,128]{2,0,1:T(8,128)(2,1)}, bf16[192,96,128]{2,0,1:T(8,128)(2,1)}, u32[]{:S(2)}, u32[]{:S(2)}) collective-permute-start(bf16[192,96,128]{2,0,1:T(8,128)(2,1)} %copy.38), channel_id=1, source_target_pairs={{0,16},{8,24},{16,0},{24,8},{1,17},{9,25},{17,1},{25,9},{2,18},{10... | collective-permute-start | bytes 14155784 | tf_op jit(solution)/shard_map/ppermute | solution.py:159
  49.7 9.8 slice-start.2
  53.7 199.7 %collective-permute-start.2 = (bf16[192,96,128]{2,0,1:T(8,128)(2,1)}, bf16[192,96,128]{2,0,1:T(8,128)(2,1)}, u32[]{:S(2)}, u32[]{:S(2)}) collective-permute-start(bf16[192,96,128]{2,0,1:T(8,128)(2,1)} %copy.39), channel_id=1, source_target_pairs={{0,24},{8,16},{16,8},{24,0},{1,25},{9,17},{17,9},{25,1},{2,26},{10... | collective-permute-start | bytes 14155784 | tf_op jit(solution)/shard_map/ppermute | solution.py:159
  53.9 5.6 slice-start.3
  57.8 296.7 %collective-permute-start.8 = (bf16[192,96,128]{2,0,1:T(8,128)(2,1)}, bf16[192,96,128]{2,0,1:T(8,128)(2,1)}, u32[]{:S(2)}, u32[]{:S(2)}) collective-permute-start(bf16[192,96,128]{2,0,1:T(8,128)(2,1)} %copy.43), channel_id=1, source_target_pairs={{0,24},{8,16},{16,8},{24,0},{1,25},{9,17},{17,9},{25,1},{2,26},{10... | collective-permute-start | bytes 14155784 | tf_op jit(solution)/shard_map/ppermute | solution.py:159
  59.4 4.2 copy-start.2
  59.4 4.2 copy-start.11
  59.4 4.2 copy-start.12
  63.4 296.9 %collective-permute-start.6 = (bf16[192,96,128]{2,0,1:T(8,128)(2,1)}, bf16[192,96,128]{2,0,1:T(8,128)(2,1)}, u32[]{:S(2)}, u32[]{:S(2)}) collective-permute-start(bf16[192,96,128]{2,0,1:T(8,128)(2,1)} %copy.41), channel_id=1, source_target_pairs={{0,8},{8,0},{16,24},{24,16},{1,9},{9,1},{17,25},{25,17},{2,10},{10... | collective-permute-start | bytes 14155784 | tf_op jit(solution)/shard_map/ppermute | solution.py:159
  80.7 274.4 %copy-start = (bf16[768,768]{0,1:T(8,128)(2,1)}, bf16[768,768]{0,1:T(8,128)(2,1)S(1)}, u32[]{:S(2)}) copy-start(bf16[768,768]{0,1:T(8,128)(2,1)S(1)} %copy.10) | copy-start | bytes 3538948
  87.1 12.8 slice-start
  93.5 6.4 slice-start.1
  103.9 352.1 %collective-permute-start.7 = (bf16[192,96,128]{2,0,1:T(8,128)(2,1)}, bf16[192,96,128]{2,0,1:T(8,128)(2,1)}, u32[]{:S(2)}, u32[]{:S(2)}) collective-permute-start(bf16[192,96,128]{2,0,1:T(8,128)(2,1)} %copy.42), channel_id=1, source_target_pairs={{0,16},{8,24},{16,0},{24,8},{1,17},{9,25},{17,1},{25,9},{2,18},{10... | collective-permute-start | bytes 14155784 | tf_op jit(solution)/shard_map/ppermute | solution.py:159
  285.3 271.4 %collective-permute-start.5 = (bf16[192,96,128]{2,0,1:T(8,128)(2,1)}, bf16[192,96,128]{2,0,1:T(8,128)(2,1)}, u32[]{:S(2)}, u32[]{:S(2)}) collective-permute-start(bf16[192,96,128]{2,0,1:T(8,128)(2,1)} %get-tuple-element.67), channel_id=1, source_target_pairs={{0,24},{8,16},{16,8},{24,0},{1,25},{9,17},{17,9},{25,1},{2,26},{10... | collective-permute-start | bytes 14155784 | tf_op jit(solution)/shard_map/ppermute | solution.py:159
  287.3 370.7 %collective-permute-start.4 = (bf16[192,96,128]{2,0,1:T(8,128)(2,1)}, bf16[192,96,128]{2,0,1:T(8,128)(2,1)}, u32[]{:S(2)}, u32[]{:S(2)}) collective-permute-start(bf16[192,96,128]{2,0,1:T(8,128)(2,1)} %get-tuple-element.68), channel_id=1, source_target_pairs={{0,16},{8,24},{16,0},{24,8},{1,17},{9,25},{17,1},{25,9},{2,18},{10... | collective-permute-start | bytes 14155784 | tf_op jit(solution)/shard_map/ppermute | solution.py:159
  354.5 311.1 %collective-permute-start.3 = (bf16[192,96,128]{2,0,1:T(8,128)(2,1)S(1)}, bf16[192,96,128]{2,0,1:T(8,128)(2,1)}, u32[]{:S(2)}, u32[]{:S(2)}) collective-permute-start(bf16[192,96,128]{2,0,1:T(8,128)(2,1)S(1)} %get-tuple-element.69), channel_id=1, source_target_pairs={{0,8},{8,0},{16,24},{24,16},{1,9},{9,1},{17,25},{25,17},{2,10},{10... | collective-permute-start | bytes 14155784 | tf_op jit(solution)/shard_map/ppermute | solution.py:159
  355.1 5.2 copy-start.1
  355.1 100.9 %copy-start.3 = (bf16[768,4,192,1]{0,2,1,3:T(8,128)(2,1)S(1)}, bf16[768,4,192,1]{0,2,1,3:T(8,128)(2,1)}, u32[]{:S(2)}) copy-start(bf16[768,4,192,1]{0,2,1,3:T(8,128)(2,1)} %reshape.70) | copy-start | bytes 3538948
  827.1 45.6 %collective-permute-start.9 = (bf16[2,96,1024]{2,1,0:T(8,128)(2,1)}, bf16[2,96,1024]{2,1,0:T(8,128)(2,1)S(1)}, u32[]{:S(2)}, u32[]{:S(2)}) collective-permute-start(bf16[2,96,1024]{2,1,0:T(8,128)(2,1)} %get-tuple-element.31), channel_id=1, source_target_pairs={{0,4},{1,5},{2,6},{3,7},{4,0},{5,1},{6,2},{7,3},{8,12},{9,13},{10,... | collective-permute-start | bytes 1179656 | tf_op jit(solution)/shard_map/ppermute | solution.py:159
  827.1 53.8 %collective-permute-start.10 = (bf16[2,96,1024]{2,1,0:T(8,128)(2,1)}, bf16[2,96,1024]{2,1,0:T(8,128)(2,1)S(1)}, u32[]{:S(2)}, u32[]{:S(2)}) collective-permute-start(bf16[2,96,1024]{2,1,0:T(8,128)(2,1)} %get-tuple-element.32), channel_id=1, source_target_pairs={{0,5},{1,4},{2,7},{3,6},{4,1},{5,0},{6,3},{7,2},{8,13},{9,12},{10,... | collective-permute-start | bytes 1179656 | tf_op jit(solution)/shard_map/ppermute | solution.py:159
  830.8 50.1 %collective-permute-start.11 = (bf16[2,96,1024]{2,1,0:T(8,128)(2,1)}, bf16[2,96,1024]{2,1,0:T(8,128)(2,1)S(1)}, u32[]{:S(2)}, u32[]{:S(2)}) collective-permute-start(bf16[2,96,1024]{2,1,0:T(8,128)(2,1)} %get-tuple-element.33), channel_id=1, source_target_pairs={{0,6},{1,7},{2,4},{3,5},{4,2},{5,3},{6,0},{7,1},{8,14},{9,15},{10,... | collective-permute-start | bytes 1179656 | tf_op jit(solution)/shard_map/ppermute | solution.py:159
  832.1 48.8 %collective-permute-start.12 = (bf16[2,96,1024]{2,1,0:T(8,128)(2,1)}, bf16[2,96,1024]{2,1,0:T(8,128)(2,1)S(1)}, u32[]{:S(2)}, u32[]{:S(2)}) collective-permute-start(bf16[2,96,1024]{2,1,0:T(8,128)(2,1)} %get-tuple-element.34), channel_id=1, source_target_pairs={{0,7},{1,6},{2,5},{3,4},{4,3},{5,2},{6,1},{7,0},{8,15},{9,14},{10,... | collective-permute-start | bytes 1179656 | tf_op jit(solution)/shard_map/ppermute | solution.py:159
  872.7 8.3 copy-start.4
  880.9 0.8 copy-start.5
  880.9 1.0 copy-start.6
  880.9 1.1 copy-start.7
  880.9 28.6 %copy-start.13 = (bf16[2,96,1024]{2,1,0:T(8,128)(2,1)S(1)}, bf16[2,96,1024]{2,1,0:T(8,128)(2,1)}, u32[]{:S(2)}) copy-start(bf16[2,96,1024]{2,1,0:T(8,128)(2,1)} %get-tuple-element.39) | copy-start | bytes 1179652
  882.0 699.9 %all-to-all-start.2 = ((bf16[160,96,1024]{2,1,0:T(8,128)(2,1)}), bf16[160,96,1024]{2,1,0:T(8,128)(2,1)}, u32[]{:S(2)}, u32[]{:S(2)}) async-start(bf16[160,96,1024]{2,1,0:T(8,128)(2,1)} %bitcast.94), calls=%async_computation.2 | async-start | bytes 62914560 | tf_op jit(solution)/shard_map/all_to_all | solution.py:225
  901.2 8.3 collective-permute-start.16
  901.3 105.0 %collective-permute-start.17 = (bf16[192,96,128]{2,0,1:T(8,128)(2,1)}, bf16[192,96,128]{2,0,1:T(8,128)(2,1)}, u32[]{:S(2)}, u32[]{:S(2)}) collective-permute-start(bf16[192,96,128]{2,0,1:T(8,128)(2,1)} %get-tuple-element.50), channel_id=1, source_target_pairs={{0,16},{8,24},{16,0},{24,8},{1,17},{9,25},{17,1},{25,9},{2,18},{10... | collective-permute-start | bytes 14155784 | tf_op jit(solution)/shard_map/ppermute | solution.py:159
  902.5 204.0 %collective-permute-start.18 = (bf16[192,96,128]{2,0,1:T(8,128)(2,1)}, bf16[192,96,128]{2,0,1:T(8,128)(2,1)}, u32[]{:S(2)}, u32[]{:S(2)}) collective-permute-start(bf16[192,96,128]{2,0,1:T(8,128)(2,1)} %get-tuple-element.51), channel_id=1, source_target_pairs={{0,24},{8,16},{16,8},{24,0},{1,25},{9,17},{17,9},{25,1},{2,26},{10... | collective-permute-start | bytes 14155784 | tf_op jit(solution)/shard_map/ppermute | solution.py:159
  903.1 259.3 %collective-permute-start.13 = (bf16[2,96,1024]{2,1,0:T(8,128)(2,1)}, bf16[2,96,1024]{2,1,0:T(8,128)(2,1)S(1)}, u32[]{:S(2)}, u32[]{:S(2)}) collective-permute-start(bf16[2,96,1024]{2,1,0:T(8,128)(2,1)} %get-tuple-element.37), channel_id=1, source_target_pairs={{0,1},{1,0},{2,3},{3,2},{4,5},{5,4},{6,7},{7,6},{8,9},{9,8},{10,11... | collective-permute-start | bytes 1179656 | tf_op jit(solution)/shard_map/ppermute | solution.py:159
  905.1 513.4 %collective-permute-start.14 = (bf16[2,96,1024]{2,1,0:T(8,128)(2,1)}, bf16[2,96,1024]{2,1,0:T(8,128)(2,1)S(1)}, u32[]{:S(2)}, u32[]{:S(2)}) collective-permute-start(bf16[2,96,1024]{2,1,0:T(8,128)(2,1)} %get-tuple-element.38), channel_id=1, source_target_pairs={{0,2},{1,3},{2,0},{3,1},{4,6},{5,7},{6,4},{7,5},{8,10},{9,11},{10,... | collective-permute-start | bytes 1179656 | tf_op jit(solution)/shard_map/ppermute | solution.py:159
  909.5 516.1 %collective-permute-start.15 = (bf16[2,96,1024]{2,1,0:T(8,128)(2,1)S(1)}, bf16[2,96,1024]{2,1,0:T(8,128)(2,1)S(1)}, u32[]{:S(2)}, u32[]{:S(2)}) collective-permute-start(bf16[2,96,1024]{2,1,0:T(8,128)(2,1)S(1)} %copy-done.13), channel_id=1, source_target_pairs={{0,3},{1,2},{2,1},{3,0},{4,7},{5,6},{6,5},{7,4},{8,11},{9,10},{10,... | collective-permute-start | bytes 1179656 | tf_op jit(solution)/shard_map/ppermute | solution.py:159
  1162.4 263.2 %copy-start.8 = (bf16[2,96,1024]{2,1,0:T(8,128)(2,1)}, bf16[2,96,1024]{2,1,0:T(8,128)(2,1)S(1)}, u32[]{:S(2)}) copy-start(bf16[2,96,1024]{2,1,0:T(8,128)(2,1)S(1)} %collective-permute-done.13.refs_1_) | copy-start | bytes 1179652
  1418.5 7.1 copy-start.9
  1425.6 0.8 copy-start.10
  1581.9 79.7 %all-to-all-start.1 = ((bf16[16,96,1024]{2,1,0:T(8,128)(2,1)}), bf16[16,96,1024]{2,1,0:T(8,128)(2,1)}, u32[]{:S(2)}, u32[]{:S(2)}) async-start(bf16[16,96,1024]{2,1,0:T(8,128)(2,1)} %bitcast.103), calls=%async_computation.1 | async-start | bytes 6291456 | tf_op jit(solution)/shard_map/all_to_all | solution.py:225

commit v4 on v3

--- a/solution.py
+++ b/solution.py
@@ -155,6 +155,82 @@
     )(place, *operands)
 
 
+def base_kernel(slabs, place_ref, operator_ref, field_ref, *refs):
+    y_refs, out_ref = refs[:-1], refs[-1]
+    parts, rows, depth, width = out_ref.shape
+    slab = width // slabs
+    share = slab // 2
+
+    def add_all(me):
+        flat = field_ref[...]
+        if depth % 16:
+            flat = flat.astype(jnp.float32)
+        flat = flat.reshape(parts * rows * depth, width).astype(jnp.bfloat16)
+        for owner in range(slabs):
+            lanes = slice(owner * slab, (owner + 1) * slab)
+            product = jnp.dot(flat, operator_ref[:, lanes], preferred_element_type=jnp.float32)
+            product = product.reshape(parts, rows, depth, slab)
+            for half in range(2):
+                here = slice(owner * slab + half * share, owner * slab + (half + 1) * share)
+                y_term = y_refs[half * slabs + (owner ^ me)][...].astype(jnp.float32)
+                x_term = product[:, :, :, half * share : (half + 1) * share]
+                out_ref[:, :, :, here] = x_term + y_term
+
+    for me in range(slabs):
+        pl.when(place_ref[0] == me)(functools.partial(add_all, me))
+
+
+def x_and_y(first, count, together, place, operator, field, y_terms):
+    parts, _, depth, width = field.shape
+    share = y_terms[0].shape[3]
+    where = lambda p, i, r: (p, i + first, 0, 0)
+    return pl.pallas_call(
+        functools.partial(base_kernel, len(y_terms) // 2),
+        grid_spec=pltpu.PrefetchScalarGridSpec(
+            num_scalar_prefetch=1,
+            grid=(parts // together, count),
+            in_specs=[
+                pl.BlockSpec((width, width), lambda p, i, r: (0, 0)),
+                pl.BlockSpec((together, 1, depth, width), where),
+            ]
+            + [pl.BlockSpec((together, 1, depth, share), where) for _ in y_terms],
+            out_specs=pl.BlockSpec((together, 1, depth, width), lambda p, i, r: (p, i, 0, 0)),
+        ),
+        out_shape=jax.ShapeDtypeStruct((parts, count, depth, width), jnp.float32),
+        compiler_params=pltpu.CompilerParams(vmem_limit_bytes=VMEM_BYTES),
+        cost_estimate=pl.CostEstimate(
+            flops=2 * width * width * parts * count * depth,
+            bytes_accessed=8 * width * parts * count * depth,
+            transcendentals=0,
+        ),
+    )(place, operator, field, *y_terms)
+
+
+def add_kernel(base_ref, z_ref, so_far_ref, out_ref):
+    out_ref[...] = (base_ref[...] + z_ref[...].astype(jnp.float32)).astype(jnp.bfloat16)
+
+
+def add_into(so_far, first, base, z_term):
+    parts, count, depth, width = z_term.shape
+    step = math.gcd(first, count)
+    skip = first // step
+    block = pl.BlockSpec((1, step, depth, width), lambda p, i: (p, i, 0, 0))
+    return pl.pallas_call(
+        add_kernel,
+        grid=(parts, count // step),
+        in_specs=[block, block, pl.BlockSpec(memory_space=pl.ANY)],
+        out_specs=pl.BlockSpec((1, step, depth, width), lambda p, i: (p, i + skip, 0, 0)),
+        out_shape=jax.ShapeDtypeStruct(so_far.shape, jnp.bfloat16),
+        input_output_aliases={2: 0},
+        compiler_params=pltpu.CompilerParams(vmem_limit_bytes=VMEM_BYTES),
+        cost_estimate=pl.CostEstimate(
+            flops=width * parts * count * depth,
+            bytes_accessed=8 * width * parts * count * depth,
+            transcendentals=0,
+        ),
+    )(base, z_term, so_far)
+
+
 def swap(value, axis, size, distance):
     return lax.ppermute(value, axis, [(i, i ^ distance) for i in range(size)])
 
@@ -237,11 +313,12 @@
 
     product = z_apply(z_transposed, planes, starts[2], sizes[2])
     result = add_chunk(None, 0, cols, z_first)
-    product, result = lax.optimization_barrier((product, result))
+    base = x_and_y(starts[2], sizes[2], cols, place, x_operator, field, y_terms)
+    product, result, base = lax.optimization_barrier((product, result, base))
     z_last = z_return(product)
 
     result = add_chunk(result, 1, cols, [z_bulk])
-    result = add_chunk(result, 2, math.gcd(cols, 4), [z_last])
+    result = add_into(result, starts[2], base, z_last)
     return result.reshape(ny, nz, nx)
 
 

time: 1670 us -> 1670 us (level)
    ppermute x19, waiting for transfers between devices: 959 us -> 938 us  [swap(): return lax.ppermute(value, axis, [(i, i ^ distance) for i in range(size)])]
    pallas_call x3 -> x2, Pallas kernels: 71.4 us -> 62.2 us  [total_into(): pl.pallas_call(functools.partial(total_kernel, len(y_terms) // 2, len(z_t...]
    unnamed x64 -> x66, local copies, waits for them, and re-layouts: 52.1 us -> 52.6 us
  transfers between devices with their start and end apart: 22 -> 22, of which waited for: 17 -> 16; matrix products, arithmetic and copies ran while one was open for 13% -> 13% of each run, Pallas kernels for 6% -> 7%
where the time goes in v4:
time: 1670 us
  waiting for transfers between devices  1270 us (76%)
  local copies, waits for them, and re-layouts  169 us (10%)
  Pallas kernels  122 us (7%)
  starting transfers between devices  61.4 us (4%)
  matrix products  41.2 us (2%)
    ppermute x19, waiting for transfers between devices, swap(): return lax.ppermute(value, axis, [(i, i ^ distance) for i in range(size)])  938 us
    all_to_all x2, waiting for transfers between devices, z_return(): return lax.all_to_all(flat, 'col', 0, 0, tiled=True).reshape(product.shape)  164 us
    all_to_all x1, waiting for transfers between devices, per_device(): planes = lax.all_to_all(scalar_field, 'col', 0, 0, tiled=True)  163 us
    pallas_call x2, Pallas kernels, total_into(): pl.pallas_call(functools.partial(total_kernel, len(y_terms) // 2, len(z_t...  62.2 us
    unnamed x66, local copies, waits for them, and re-layouts  52.6 us
    ppermute x6, local copies, waits for them, and re-layouts, swap(): return lax.ppermute(value, axis, [(i, i ^ distance) for i in range(size)])  45.4 us
    dot_general x2, matrix products, y_multiply(): jnp.einsum('yzx,ydk->dkzx', pencil, by_distance, preferred_element_type=j...  41.2 us
    pallas_call x2, Pallas kernels, z_apply(): pl.pallas_call(z_kernel, grid=(count // step,), in_specs=[pl.BlockSpec((p...  38.6 us
  transfers between devices with their start and end apart: 22, of which 16 were waited for; matrix products, arithmetic and copies ran while one was open for 13% of the time, Pallas kernels for 7%

profile of v4, /device:TPU:0, one launch (start us, length us, event | category | flops | bytes accessed | tf_op | source)
XLA Modules:
  0.0 1669.1 jit_solution(1929666049193453519)
XLA Ops:
  0.0 7.5 all-to-all-start
  7.6 26.3 %constant_dynamic-slice_fusion.3 = (bf16[192,96,128]{2,1,0:T(8,128)(2,1)}, bf16[192,96,128]{2,1,0:T(8,128)(2,1)}, bf16[192,96,128]{2,1,0:T(8,128)(2,1)}, bf16[19...) fusion(bf16[192,96,1024]{2,1,0:T(8,128)(2,1)} %param.7, ...), kind=kLoop, calls=%fused_computation.41 | loop fusion | bytes 75497504 | tf_op jit(solution)/shard_map/dynamic_slice | solution.py:265
  33.8 6.4 copy.39
  40.2 2.4 collective-permute-start.2
  42.6 6.6 copy.38
  49.7 4.0 copy.37
  53.9 3.9 copy.43
  57.8 1.4 collective-permute-start.8
  59.3 3.9 copy.42
  63.8 1.7 add_convert_fusion
  67.5 1.9 copy.35
  69.4 1.7 copy.34
  71.2 1.7 copy.33
  72.9 1.7 copy.32
  74.6 4.1 pad_maximum_fusion
  79.3 1.6 copy.10
  80.9 6.8 copy.36
  87.7 2.4 pad_maximum_fusion.1
  90.1 4.1 reshape.70
  94.2 6.5 copy.41
  100.6 4.0 copy.40
  104.7 40.5 %collective-permute-done.2 = bf16[192,96,128]{2,0,1:T(8,128)(2,1)} collective-permute-done((bf16[192,96,128]{2,0,1:T(8,128)(2,1)}, bf16[192,96,128]{2,0,1:T(8,128)(2,1)}, u32[]{:S(2)}, u32[]{:S(2)}) %collective-permute-start.2) | collective-permute-done | bytes 4718624 | tf_op jit(solution)/shard_map/ppermute | solution.py:235
  146.3 101.0 %collective-permute-done.1 = bf16[192,96,128]{2,0,1:T(8,128)(2,1)} collective-permute-done((bf16[192,96,128]{2,0,1:T(8,128)(2,1)}, bf16[192,96,128]{2,0,1:T(8,128)(2,1)}, u32[]{:S(2)}, u32[]{:S(2)}) %collective-permute-start.1) | collective-permute-done | bytes 4718624 | tf_op jit(solution)/shard_map/ppermute | solution.py:235
  247.2 20.9 %fusion.15 = bf16[4,192,96,128]{3,1,2,0:T(8,128)(2,1)} fusion(bf16[192,96,128]{2,0,1:T(8,128)(2,1)} %collective-permute-done.2, bf16[192,96,128]{2,0,1:T(8,128)(2,1)} %collective-permute-done.1, bf16[192,96,128]{2,0,1:T(8,128)(2,1)} %collective-permute-done, bf16[192,96,128]{2,0,1:T(8,128)(2,1)} %copy.36, bf16[768,4,192,1]{0,2,1,3:T(8,128)(2,1)} %reshape.70), kind=kOutput, calls=%fused_computation.17 | convolution fusion | flops 14580449280 | bytes 38928384 | tf_op jit(solution)/shard_map/yzx,ydk->dkzx/dot_general | solution.py:270
  268.2 11.1 slice_bitcast_fusion.4
  279.2 1.6 collective-permute-start.4
  280.8 66.5 %collective-permute-done.8 = bf16[192,96,128]{2,0,1:T(8,128)(2,1)} collective-permute-done((bf16[192,96,128]{2,0,1:T(8,128)(2,1)}, bf16[192,96,128]{2,0,1:T(8,128)(2,1)}, u32[]{:S(2)}, u32[]{:S(2)}) %collective-permute-start.8) | collective-permute-done | bytes 4718624 | tf_op jit(solution)/shard_map/ppermute | solution.py:235
  347.4 2.2 collective-permute-start.5
  349.7 5.2 copy.19
  354.9 94.6 %collective-permute-done.7 = bf16[192,96,128]{2,0,1:T(8,128)(2,1)} collective-permute-done((bf16[192,96,128]{2,0,1:T(8,128)(2,1)}, bf16[192,96,128]{2,0,1:T(8,128)(2,1)}, u32[]{:S(2)}, u32[]{:S(2)}) %collective-permute-start.7) | collective-permute-done | bytes 4718624 | tf_op jit(solution)/shard_map/ppermute | solution.py:235
  449.5 20.3 %fusion.14 = bf16[4,192,96,128]{3,1,2,0:T(8,128)(2,1)} fusion(bf16[192,96,128]{2,0,1:T(8,128)(2,1)} %collective-permute-done.8, bf16[192,96,128]{2,0,1:T(8,128)(2,1)} %collective-permute-done.7, bf16[192,96,128]{2,0,1:T(8,128)(2,1)} %collective-permute-done.6, bf16[192,96,128]{2,0,1:T(8,128)(2,1)} %copy.40, bf16[768,4,192,1]{0,2,1,3:T(8,128)(2,1)S(1)} %copy-done.3), kind=kOutput, calls=%fused_computation.16 | convolution fusion | flops 14580449280 | bytes 38928384 | tf_op jit(solution)/shard_map/yzx,ydk->dkzx/dot_general | solution.py:270
  469.8 13.9 slice_bitcast_fusion
  483.7 7.5 copy.20
  491.2 59.4 %collective-permute-done.4 = bf16[192,96,128]{2,0,1:T(8,128)(2,1)} collective-permute-done((bf16[192,96,128]{2,0,1:T(8,128)(2,1)}, bf16[192,96,128]{2,0,1:T(8,128)(2,1)}, u32[]{:S(2)}, u32[]{:S(2)}) %collective-permute-start.4) | collective-permute-done | bytes 4718624 | tf_op jit(solution)/shard_map/ppermute | solution.py:235
  550.6 7.6 copy.21
  558.2 92.4 %collective-permute-done.5 = bf16[192,96,128]{2,0,1:T(8,128)(2,1)} collective-permute-done((bf16[192,96,128]{2,0,1:T(8,128)(2,1)S(1)}, bf16[192,96,128]{2,0,1:T(8,128)(2,1)}, u32[]{:S(2)}, u32[]{:S(2)}) %collective-permute-start.5) | collective-permute-done | bytes 4718624 | tf_op jit(solution)/shard_map/ppermute | solution.py:235
  650.6 7.5 copy.22
  658.1 163.4 %all-to-all-done = bf16[192,96,1024]{2,1,0:T(8,128)(2,1)} async-done(((bf16[192,96,1024]{2,1,0:T(8,128)(2,1)}), bf16[192,96,1024]{2,1,0:T(8,128)(2,1)}, u32[]{:S(2)}, u32[]{:S(2)}) %all-to-all-start) | async-done | bytes 37748768 | tf_op jit(solution)/shard_map/all_to_all | solution.py:253
  821.5 5.5 shard_map.74
  827.1 3.8 collective-permute-start.10
  832.1 2.6 collective-permute-start.12
  834.7 32.1 %shard_map.73 = bf16[8,20,96,1024]{3,2,1,0:T(8,128)(2,1)} custom-call(bf16[768,768]{1,0:T(8,128)(2,1)} %bitcast.112, bf16[8,24,96,1024]{3,2,1,0:T(8,128)(2,1)} %bitcast.15.field_ref), custom_call_target="tpu_custom_call" | custom-call | flops 24159191040 | bytes 62914560 | tf_op jit(solution)/shard_map/pallas_call | solution.py:30
  866.8 5.8 collective-permute-done.9.refs_4_
  872.7 8.2 collective-permute-done.10.refs_5_
  881.9 19.2 %all-to-all-start.2 = ((bf16[160,96,1024]{2,1,0:T(8,128)(2,1)}), bf16[160,96,1024]{2,1,0:T(8,128)(2,1)}, u32[]{:S(2)}, u32[]{:S(2)}) async-start(bf16[160,96,1024]{2,1,0:T(8,128)(2,1)} %bitcast.94), calls=%async_computation.2 | async-start | bytes 62914560 | tf_op jit(solution)/shard_map/all_to_all | solution.py:301
  903.8 2.0 collective-permute-start.13
  905.8 4.2 collective-permute-start.14
  910.0 7.6 copy.27
  917.9 6.5 shard_map.75
  924.4 7.5 copy.28
  931.9 74.3 %collective-permute-done.17 = bf16[192,96,128]{2,0,1:T(8,128)(2,1)} collective-permute-done((bf16[192,96,128]{2,0,1:T(8,128)(2,1)}, bf16[192,96,128]{2,0,1:T(8,128)(2,1)}, u32[]{:S(2)}, u32[]{:S(2)}) %collective-permute-start.17) | collective-permute-done | bytes 4718624 | tf_op jit(solution)/shard_map/ppermute | solution.py:235
  1006.2 7.5 copy.29
  1013.7 92.8 %collective-permute-done.18 = bf16[192,96,128]{2,0,1:T(8,128)(2,1)} collective-permute-done((bf16[192,96,128]{2,0,1:T(8,128)(2,1)}, bf16[192,96,128]{2,0,1:T(8,128)(2,1)}, u32[]{:S(2)}, u32[]{:S(2)}) %collective-permute-start.18) | collective-permute-done | bytes 4718624 | tf_op jit(solution)/shard_map/ppermute | solution.py:235
  1106.4 7.9 copy.30
  1114.3 8.7 shard_map.77.base_ref
  1123.0 39.4 %collective-permute-done.13.refs_1_ = bf16[2,96,1024]{2,1,0:T(8,128)(2,1)S(1)} collective-permute-done((bf16[2,96,1024]{2,1,0:T(8,128)(2,1)}, bf16[2,96,1024]{2,1,0:T(8,128)(2,1)S(1)}, u32[]{:S(2)}, u32[]{:S(2)}) %collective-permute-start.13) | collective-permute-done | bytes 393248 | tf_op jit(solution)/shard_map/ppermute | solution.py:235
  1162.3 256.1 %collective-permute-done.14.refs_2_ = bf16[2,96,1024]{2,1,0:T(8,128)(2,1)S(1)} collective-permute-done((bf16[2,96,1024]{2,1,0:T(8,128)(2,1)S(1)}, bf16[2,96,1024]{2,1,0:T(8,128)(2,1)S(1)}, u32[]{:S(2)}, u32[]{:S(2)}) %collective-permute-start.14) | collective-permute-done | bytes 393248 | tf_op jit(solution)/shard_map/ppermute | solution.py:235
  1418.4 7.2 collective-permute-done.15.refs_3_
  1426.3 9.2 shard_map.76.refs_9_
  1435.5 146.4 %all-to-all-done.2 = bf16[160,96,1024]{2,1,0:T(8,128)(2,1)} async-done(((bf16[160,96,1024]{2,1,0:T(8,128)(2,1)}), bf16[160,96,1024]{2,1,0:T(8,128)(2,1)}, u32[]{:S(2)}, u32[]{:S(2)}) %all-to-all-start.2) | async-done | bytes 31457312 | tf_op jit(solution)/shard_map/all_to_all | solution.py:301
  1581.9 8.5 all-to-all-start.1
  1590.4 53.0 %shard_map.78.so_far_ref = bf16[8,24,96,1024]{3,2,1,0:T(8,128)(2,1)} custom-call(s32[2]{0:T(128)} %pad_add_fusion.place_ref, bf16[1024,1024]{1,0:T(8,128)(2,1)} %operator_ref.5, bf16[8,24,96,1024]{3,2,1,0:T(8,128)(2,1)} %bitcast.69, bf16[8,20,96,1024]{3,2,1,0:T(8,128)(2,1)} %bitcast.36.refs_0_, ...), custom_call_target="tpu_custom_call", output_to_operand_aliasing={{}: (12, {})} | custom-call | flops 32212254720 | bytes 125829120 | tf_op jit(solution)/shard_map/pallas_call | solution.py:138
  1643.4 18.0 %all-to-all-done.1 = bf16[16,96,1024]{2,1,0:T(8,128)(2,1)} async-done(((bf16[16,96,1024]{2,1,0:T(8,128)(2,1)}), bf16[16,96,1024]{2,1,0:T(8,128)(2,1)}, u32[]{:S(2)}, u32[]{:S(2)}) %all-to-all-start.1) | async-done | bytes 3145760 | tf_op jit(solution)/shard_map/all_to_all | solution.py:301
  1661.4 7.5 shard_map.79
  (79 shorter events, 11.1 us)
Async XLA Ops:
  0.0 821.5 %all-to-all-start = ((bf16[192,96,1024]{2,1,0:T(8,128)(2,1)}), bf16[192,96,1024]{2,1,0:T(8,128)(2,1)}, u32[]{:S(2)}, u32[]{:S(2)}) async-start(bf16[192,96,1024]{2,1,0:T(8,128)(2,1)} %param.7), calls=%async_computation | async-start | bytes 75497472 | tf_op jit(solution)/shard_map/all_to_all | solution.py:253
  33.8 15.9 slice-start.6
  33.8 20.1 %slice-start.4 = ((s8[4718592]{0:T(1024)(128)(4,1)}), s8[4194304]{0:T(1024)(128)(4,1)S(1)}, s32[]{:S(2)}) async-start(s8[4718592]{0:T(1024)(128)(4,1)} %bitcast.99), calls=%async_computation.7 | async-start | bytes 8388608
  40.2 104.9 %collective-permute-start.2 = (bf16[192,96,128]{2,0,1:T(8,128)(2,1)}, bf16[192,96,128]{2,0,1:T(8,128)(2,1)}, u32[]{:S(2)}, u32[]{:S(2)}) collective-permute-start(bf16[192,96,128]{2,0,1:T(8,128)(2,1)} %copy.39), channel_id=1, source_target_pairs={{0,24},{8,16},{16,8},{24,0},{1,25},{9,17},{17,9},{25,1},{2,26},{10... | collective-permute-start | bytes 14155784 | tf_op jit(solution)/shard_map/ppermute | solution.py:235
  42.6 7.1 slice-start.7
  42.6 11.3 slice-start.5
  49.2 198.1 %collective-permute-start.1 = (bf16[192,96,128]{2,0,1:T(8,128)(2,1)}, bf16[192,96,128]{2,0,1:T(8,128)(2,1)}, u32[]{:S(2)}, u32[]{:S(2)}) collective-permute-start(bf16[192,96,128]{2,0,1:T(8,128)(2,1)} %copy.38), channel_id=1, source_target_pairs={{0,16},{8,24},{16,0},{24,8},{1,17},{9,25},{17,1},{25,9},{2,18},{10... | collective-permute-start | bytes 14155784 | tf_op jit(solution)/shard_map/ppermute | solution.py:235
  49.7 9.5 slice-start.2
  53.8 193.5 %collective-permute-start = (bf16[192,96,128]{2,0,1:T(8,128)(2,1)}, bf16[192,96,128]{2,0,1:T(8,128)(2,1)}, u32[]{:S(2)}, u32[]{:S(2)}) collective-permute-start(bf16[192,96,128]{2,0,1:T(8,128)(2,1)} %copy.37), channel_id=1, source_target_pairs={{0,8},{8,0},{16,24},{24,16},{1,9},{9,1},{17,25},{25,17},{2,10},{10... | collective-permute-start | bytes 14155784 | tf_op jit(solution)/shard_map/ppermute | solution.py:235
  53.9 5.4 slice-start.3
  57.8 289.5 %collective-permute-start.8 = (bf16[192,96,128]{2,0,1:T(8,128)(2,1)}, bf16[192,96,128]{2,0,1:T(8,128)(2,1)}, u32[]{:S(2)}, u32[]{:S(2)}) collective-permute-start(bf16[192,96,128]{2,0,1:T(8,128)(2,1)} %copy.43), channel_id=1, source_target_pairs={{0,24},{8,16},{16,8},{24,0},{1,25},{9,17},{17,9},{25,1},{2,26},{10... | collective-permute-start | bytes 14155784 | tf_op jit(solution)/shard_map/ppermute | solution.py:235
  59.3 4.5 copy-start.2
  59.3 4.5 copy-start.11
  59.3 4.5 copy-start.12
  63.2 386.2 %collective-permute-start.7 = (bf16[192,96,128]{2,0,1:T(8,128)(2,1)}, bf16[192,96,128]{2,0,1:T(8,128)(2,1)}, u32[]{:S(2)}, u32[]{:S(2)}) collective-permute-start(bf16[192,96,128]{2,0,1:T(8,128)(2,1)} %copy.42), channel_id=1, source_target_pairs={{0,16},{8,24},{16,0},{24,8},{1,17},{9,25},{17,1},{25,9},{2,18},{10... | collective-permute-start | bytes 14155784 | tf_op jit(solution)/shard_map/ppermute | solution.py:235
  80.9 268.8 %copy-start = (bf16[768,768]{0,1:T(8,128)(2,1)}, bf16[768,768]{0,1:T(8,128)(2,1)S(1)}, u32[]{:S(2)}) copy-start(bf16[768,768]{0,1:T(8,128)(2,1)S(1)} %copy.10) | copy-start | bytes 3538948
  90.1 10.6 slice-start
  94.2 6.5 slice-start.1
  145.1 304.4 %collective-permute-start.6 = (bf16[192,96,128]{2,0,1:T(8,128)(2,1)}, bf16[192,96,128]{2,0,1:T(8,128)(2,1)}, u32[]{:S(2)}, u32[]{:S(2)}) collective-permute-start(bf16[192,96,128]{2,0,1:T(8,128)(2,1)} %copy.41), channel_id=1, source_target_pairs={{0,8},{8,0},{16,24},{24,16},{1,9},{9,1},{17,25},{25,17},{2,10},{10... | collective-permute-start | bytes 14155784 | tf_op jit(solution)/shard_map/ppermute | solution.py:235
  279.2 204.4 %collective-permute-start.3 = (bf16[192,96,128]{2,0,1:T(8,128)(2,1)}, bf16[192,96,128]{2,0,1:T(8,128)(2,1)}, u32[]{:S(2)}, u32[]{:S(2)}) collective-permute-start(bf16[192,96,128]{2,0,1:T(8,128)(2,1)} %get-tuple-element.71), channel_id=1, source_target_pairs={{0,8},{8,0},{16,24},{24,16},{1,9},{9,1},{17,25},{25,17},{2,10},{10... | collective-permute-start | bytes 14155784 | tf_op jit(solution)/shard_map/ppermute | solution.py:235
  279.2 271.3 %collective-permute-start.4 = (bf16[192,96,128]{2,0,1:T(8,128)(2,1)}, bf16[192,96,128]{2,0,1:T(8,128)(2,1)}, u32[]{:S(2)}, u32[]{:S(2)}) collective-permute-start(bf16[192,96,128]{2,0,1:T(8,128)(2,1)} %get-tuple-element.70), channel_id=1, source_target_pairs={{0,16},{8,24},{16,0},{24,8},{1,17},{9,25},{17,1},{25,9},{2,18},{10... | collective-permute-start | bytes 14155784 | tf_op jit(solution)/shard_map/ppermute | solution.py:235
  347.4 303.2 %collective-permute-start.5 = (bf16[192,96,128]{2,0,1:T(8,128)(2,1)S(1)}, bf16[192,96,128]{2,0,1:T(8,128)(2,1)}, u32[]{:S(2)}, u32[]{:S(2)}) collective-permute-start(bf16[192,96,128]{2,0,1:T(8,128)(2,1)S(1)} %get-tuple-element.69), channel_id=1, source_target_pairs={{0,24},{8,16},{16,8},{24,0},{1,25},{9,17},{17,9},{25,1},{2,26},{10... | collective-permute-start | bytes 14155784 | tf_op jit(solution)/shard_map/ppermute | solution.py:235
  349.7 5.2 copy-start.1
  349.7 99.8 %copy-start.3 = (bf16[768,4,192,1]{0,2,1,3:T(8,128)(2,1)S(1)}, bf16[768,4,192,1]{0,2,1,3:T(8,128)(2,1)}, u32[]{:S(2)}) copy-start(bf16[768,4,192,1]{0,2,1,3:T(8,128)(2,1)} %reshape.70) | copy-start | bytes 3538948
  827.1 45.6 %collective-permute-start.9 = (bf16[2,96,1024]{2,1,0:T(8,128)(2,1)}, bf16[2,96,1024]{2,1,0:T(8,128)(2,1)S(1)}, u32[]{:S(2)}, u32[]{:S(2)}) collective-permute-start(bf16[2,96,1024]{2,1,0:T(8,128)(2,1)} %get-tuple-element.32), channel_id=1, source_target_pairs={{0,4},{1,5},{2,6},{3,7},{4,0},{5,1},{6,2},{7,3},{8,12},{9,13},{10,... | collective-permute-start | bytes 1179656 | tf_op jit(solution)/shard_map/ppermute | solution.py:235
  827.1 53.8 %collective-permute-start.10 = (bf16[2,96,1024]{2,1,0:T(8,128)(2,1)}, bf16[2,96,1024]{2,1,0:T(8,128)(2,1)S(1)}, u32[]{:S(2)}, u32[]{:S(2)}) collective-permute-start(bf16[2,96,1024]{2,1,0:T(8,128)(2,1)} %get-tuple-element.33), channel_id=1, source_target_pairs={{0,5},{1,4},{2,7},{3,6},{4,1},{5,0},{6,3},{7,2},{8,13},{9,12},{10,... | collective-permute-start | bytes 1179656 | tf_op jit(solution)/shard_map/ppermute | solution.py:235
  830.8 50.1 %collective-permute-start.11 = (bf16[2,96,1024]{2,1,0:T(8,128)(2,1)}, bf16[2,96,1024]{2,1,0:T(8,128)(2,1)S(1)}, u32[]{:S(2)}, u32[]{:S(2)}) collective-permute-start(bf16[2,96,1024]{2,1,0:T(8,128)(2,1)} %get-tuple-element.34), channel_id=1, source_target_pairs={{0,6},{1,7},{2,4},{3,5},{4,2},{5,3},{6,0},{7,1},{8,14},{9,15},{10,... | collective-permute-start | bytes 1179656 | tf_op jit(solution)/shard_map/ppermute | solution.py:235
  832.1 48.8 %collective-permute-start.12 = (bf16[2,96,1024]{2,1,0:T(8,128)(2,1)}, bf16[2,96,1024]{2,1,0:T(8,128)(2,1)S(1)}, u32[]{:S(2)}, u32[]{:S(2)}) collective-permute-start(bf16[2,96,1024]{2,1,0:T(8,128)(2,1)} %get-tuple-element.35), channel_id=1, source_target_pairs={{0,7},{1,6},{2,5},{3,4},{4,3},{5,2},{6,1},{7,0},{8,15},{9,14},{10,... | collective-permute-start | bytes 1179656 | tf_op jit(solution)/shard_map/ppermute | solution.py:235
  872.7 8.3 copy-start.4
  880.9 0.8 copy-start.5
  880.9 0.9 copy-start.6
  880.9 1.0 copy-start.7
  880.9 24.9 %copy-start.14 = (bf16[2,96,1024]{2,1,0:T(8,128)(2,1)S(1)}, bf16[2,96,1024]{2,1,0:T(8,128)(2,1)}, u32[]{:S(2)}) copy-start(bf16[2,96,1024]{2,1,0:T(8,128)(2,1)} %get-tuple-element.39) | copy-start | bytes 1179652
  881.9 700.0 %all-to-all-start.2 = ((bf16[160,96,1024]{2,1,0:T(8,128)(2,1)}), bf16[160,96,1024]{2,1,0:T(8,128)(2,1)}, u32[]{:S(2)}, u32[]{:S(2)}) async-start(bf16[160,96,1024]{2,1,0:T(8,128)(2,1)} %bitcast.94), calls=%async_computation.2 | async-start | bytes 62914560 | tf_op jit(solution)/shard_map/all_to_all | solution.py:301
  901.1 16.4 collective-permute-start.16
  901.2 105.0 %collective-permute-start.17 = (bf16[192,96,128]{2,0,1:T(8,128)(2,1)}, bf16[192,96,128]{2,0,1:T(8,128)(2,1)}, u32[]{:S(2)}, u32[]{:S(2)}) collective-permute-start(bf16[192,96,128]{2,0,1:T(8,128)(2,1)} %get-tuple-element.51), channel_id=1, source_target_pairs={{0,16},{8,24},{16,0},{24,8},{1,17},{9,25},{17,1},{25,9},{2,18},{10... | collective-permute-start | bytes 14155784 | tf_op jit(solution)/shard_map/ppermute | solution.py:235
  902.4 204.0 %collective-permute-start.18 = (bf16[192,96,128]{2,0,1:T(8,128)(2,1)}, bf16[192,96,128]{2,0,1:T(8,128)(2,1)}, u32[]{:S(2)}, u32[]{:S(2)}) collective-permute-start(bf16[192,96,128]{2,0,1:T(8,128)(2,1)} %get-tuple-element.52), channel_id=1, source_target_pairs={{0,24},{8,16},{16,8},{24,0},{1,25},{9,17},{17,9},{25,1},{2,26},{10... | collective-permute-start | bytes 14155784 | tf_op jit(solution)/shard_map/ppermute | solution.py:235
  903.8 258.6 %collective-permute-start.13 = (bf16[2,96,1024]{2,1,0:T(8,128)(2,1)}, bf16[2,96,1024]{2,1,0:T(8,128)(2,1)S(1)}, u32[]{:S(2)}, u32[]{:S(2)}) collective-permute-start(bf16[2,96,1024]{2,1,0:T(8,128)(2,1)} %get-tuple-element.38), channel_id=1, source_target_pairs={{0,1},{1,0},{2,3},{3,2},{4,5},{5,4},{6,7},{7,6},{8,9},{9,8},{10,11... | collective-permute-start | bytes 1179656 | tf_op jit(solution)/shard_map/ppermute | solution.py:235
  905.8 11.8 copy-start.13
  905.8 512.6 %collective-permute-start.14 = (bf16[2,96,1024]{2,1,0:T(8,128)(2,1)S(1)}, bf16[2,96,1024]{2,1,0:T(8,128)(2,1)S(1)}, u32[]{:S(2)}, u32[]{:S(2)}) collective-permute-start(bf16[2,96,1024]{2,1,0:T(8,128)(2,1)S(1)} %copy-done.14), channel_id=1, source_target_pairs={{0,2},{1,3},{2,0},{3,1},{4,6},{5,7},{6,4},{7,5},{8,10},{9,11},{10,... | collective-permute-start | bytes 1179656 | tf_op jit(solution)/shard_map/ppermute | solution.py:235
  917.5 508.0 %collective-permute-start.15 = (bf16[2,96,1024]{2,1,0:T(8,128)(2,1)S(1)}, bf16[2,96,1024]{2,1,0:T(8,128)(2,1)S(1)}, u32[]{:S(2)}, u32[]{:S(2)}) collective-permute-start(bf16[2,96,1024]{2,1,0:T(8,128)(2,1)S(1)} %copy-done.13), channel_id=1, source_target_pairs={{0,3},{1,2},{2,1},{3,0},{4,7},{5,6},{6,5},{7,4},{8,11},{9,10},{10,... | collective-permute-start | bytes 1179656 | tf_op jit(solution)/shard_map/ppermute | solution.py:235
  1162.3 263.2 %copy-start.8 = (bf16[2,96,1024]{2,1,0:T(8,128)(2,1)}, bf16[2,96,1024]{2,1,0:T(8,128)(2,1)S(1)}, u32[]{:S(2)}) copy-start(bf16[2,96,1024]{2,1,0:T(8,128)(2,1)S(1)} %collective-permute-done.13.refs_1_) | copy-start | bytes 1179652
  1418.4 7.2 copy-start.9
  1425.6 0.8 copy-start.10
  1581.9 79.5 %all-to-all-start.1 = ((bf16[16,96,1024]{2,1,0:T(8,128)(2,1)}), bf16[16,96,1024]{2,1,0:T(8,128)(2,1)}, u32[]{:S(2)}, u32[]{:S(2)}) async-start(bf16[16,96,1024]{2,1,0:T(8,128)(2,1)} %bitcast.103), calls=%async_computation.1 | async-start | bytes 6291456 | tf_op jit(solution)/shard_map/all_to_all | solution.py:301

commit v5 on v4

--- a/solution.py
+++ b/solution.py
@@ -214,12 +214,13 @@
     parts, count, depth, width = z_term.shape
     step = math.gcd(first, count)
     skip = first // step
-    block = pl.BlockSpec((1, step, depth, width), lambda p, i: (p, i, 0, 0))
+    together = math.gcd(parts, 4)
+    block = pl.BlockSpec((together, step, depth, width), lambda p, i: (p, i, 0, 0))
     return pl.pallas_call(
         add_kernel,
-        grid=(parts, count // step),
+        grid=(parts // together, count // step),
         in_specs=[block, block, pl.BlockSpec(memory_space=pl.ANY)],
-        out_specs=pl.BlockSpec((1, step, depth, width), lambda p, i: (p, i + skip, 0, 0)),
+        out_specs=pl.BlockSpec((together, step, depth, width), lambda p, i: (p, i + skip, 0, 0)),
         out_shape=jax.ShapeDtypeStruct(so_far.shape, jnp.bfloat16),
         input_output_aliases={2: 0},
         compiler_params=pltpu.CompilerParams(vmem_limit_bytes=VMEM_BYTES),

time: 1670 us -> 1670 us (level)
  no operation moved by 1% of the time
where the time goes in v5:
time: 1670 us
  waiting for transfers between devices  1270 us (76%)
  local copies, waits for them, and re-layouts  169 us (10%)
  Pallas kernels  120 us (7%)
  starting transfers between devices  61.4 us (4%)
  matrix products  41.2 us (2%)
    ppermute x19, waiting for transfers between devices, swap(): return lax.ppermute(value, axis, [(i, i ^ distance) for i in range(size)])  938 us
    all_to_all x2, waiting for transfers between devices, z_return(): return lax.all_to_all(flat, 'col', 0, 0, tiled=True).reshape(product.shape)  164 us
    all_to_all x1, waiting for transfers between devices, per_device(): planes = lax.all_to_all(scalar_field, 'col', 0, 0, tiled=True)  163 us
    pallas_call x2, Pallas kernels, total_into(): pl.pallas_call(functools.partial(total_kernel, len(y_terms) // 2, len(z_t...  62.2 us
    unnamed x66, local copies, waits for them, and re-layouts  52.6 us
    ppermute x6, local copies, waits for them, and re-layouts, swap(): return lax.ppermute(value, axis, [(i, i ^ distance) for i in range(size)])  45.4 us
    dot_general x2, matrix products, y_multiply(): jnp.einsum('yzx,ydk->dkzx', pencil, by_distance, preferred_element_type=j...  41.2 us
    pallas_call x2, Pallas kernels, z_apply(): pl.pallas_call(z_kernel, grid=(count // step,), in_specs=[pl.BlockSpec((p...  38.6 us
  transfers between devices with their start and end apart: 22, of which 16 were waited for; matrix products, arithmetic and copies ran while one was open for 13% of the time, Pallas kernels for 7%

profile of v5, /device:TPU:0, one launch (start us, length us, event | category | flops | bytes accessed | tf_op | source)
XLA Modules:
  0.0 1667.1 jit_solution(614446420710256734)
XLA Ops:
  0.0 7.5 all-to-all-start
  7.6 26.3 %constant_dynamic-slice_fusion.3 = (bf16[192,96,128]{2,1,0:T(8,128)(2,1)}, bf16[192,96,128]{2,1,0:T(8,128)(2,1)}, bf16[192,96,128]{2,1,0:T(8,128)(2,1)}, bf16[19...) fusion(bf16[192,96,1024]{2,1,0:T(8,128)(2,1)} %param.7, ...), kind=kLoop, calls=%fused_computation.41 | loop fusion | bytes 75497504 | tf_op jit(solution)/shard_map/dynamic_slice | solution.py:266
  33.8 6.4 copy.39
  40.2 2.4 collective-permute-start.2
  42.6 6.6 copy.38
  49.7 4.0 copy.37
  53.9 3.9 copy.43
  57.8 1.4 collective-permute-start.8
  59.3 3.9 copy.42
  63.8 1.7 add_convert_fusion
  67.5 1.9 copy.35
  69.4 1.7 copy.34
  71.2 1.7 copy.33
  72.9 1.7 copy.32
  74.6 4.1 pad_maximum_fusion
  79.3 1.6 copy.10
  80.9 6.8 copy.36
  87.7 2.4 pad_maximum_fusion.1
  90.1 4.1 reshape.70
  94.2 6.5 copy.41
  100.6 4.0 copy.40
  104.7 40.5 %collective-permute-done.2 = bf16[192,96,128]{2,0,1:T(8,128)(2,1)} collective-permute-done((bf16[192,96,128]{2,0,1:T(8,128)(2,1)}, bf16[192,96,128]{2,0,1:T(8,128)(2,1)}, u32[]{:S(2)}, u32[]{:S(2)}) %collective-permute-start.2) | collective-permute-done | bytes 4718624 | tf_op jit(solution)/shard_map/ppermute | solution.py:236
  146.3 101.0 %collective-permute-done.1 = bf16[192,96,128]{2,0,1:T(8,128)(2,1)} collective-permute-done((bf16[192,96,128]{2,0,1:T(8,128)(2,1)}, bf16[192,96,128]{2,0,1:T(8,128)(2,1)}, u32[]{:S(2)}, u32[]{:S(2)}) %collective-permute-start.1) | collective-permute-done | bytes 4718624 | tf_op jit(solution)/shard_map/ppermute | solution.py:236
  247.2 20.9 %fusion.15 = bf16[4,192,96,128]{3,1,2,0:T(8,128)(2,1)} fusion(bf16[192,96,128]{2,0,1:T(8,128)(2,1)} %collective-permute-done.2, bf16[192,96,128]{2,0,1:T(8,128)(2,1)} %collective-permute-done.1, bf16[192,96,128]{2,0,1:T(8,128)(2,1)} %collective-permute-done, bf16[192,96,128]{2,0,1:T(8,128)(2,1)} %copy.36, bf16[768,4,192,1]{0,2,1,3:T(8,128)(2,1)} %reshape.70), kind=kOutput, calls=%fused_computation.17 | convolution fusion | flops 14580449280 | bytes 38928384 | tf_op jit(solution)/shard_map/yzx,ydk->dkzx/dot_general | solution.py:271
  268.2 11.1 slice_bitcast_fusion.4
  279.2 1.6 collective-permute-start.4
  280.8 66.5 %collective-permute-done.8 = bf16[192,96,128]{2,0,1:T(8,128)(2,1)} collective-permute-done((bf16[192,96,128]{2,0,1:T(8,128)(2,1)}, bf16[192,96,128]{2,0,1:T(8,128)(2,1)}, u32[]{:S(2)}, u32[]{:S(2)}) %collective-permute-start.8) | collective-permute-done | bytes 4718624 | tf_op jit(solution)/shard_map/ppermute | solution.py:236
  347.4 2.2 collective-permute-start.5
  349.7 5.2 copy.19
  354.9 94.6 %collective-permute-done.7 = bf16[192,96,128]{2,0,1:T(8,128)(2,1)} collective-permute-done((bf16[192,96,128]{2,0,1:T(8,128)(2,1)}, bf16[192,96,128]{2,0,1:T(8,128)(2,1)}, u32[]{:S(2)}, u32[]{:S(2)}) %collective-permute-start.7) | collective-permute-done | bytes 4718624 | tf_op jit(solution)/shard_map/ppermute | solution.py:236
  449.5 20.3 %fusion.14 = bf16[4,192,96,128]{3,1,2,0:T(8,128)(2,1)} fusion(bf16[192,96,128]{2,0,1:T(8,128)(2,1)} %collective-permute-done.8, bf16[192,96,128]{2,0,1:T(8,128)(2,1)} %collective-permute-done.7, bf16[192,96,128]{2,0,1:T(8,128)(2,1)} %collective-permute-done.6, bf16[192,96,128]{2,0,1:T(8,128)(2,1)} %copy.40, bf16[768,4,192,1]{0,2,1,3:T(8,128)(2,1)S(1)} %copy-done.3), kind=kOutput, calls=%fused_computation.16 | convolution fusion | flops 14580449280 | bytes 38928384 | tf_op jit(solution)/shard_map/yzx,ydk->dkzx/dot_general | solution.py:271
  469.8 13.9 slice_bitcast_fusion
  483.7 7.5 copy.20
  491.2 59.4 %collective-permute-done.4 = bf16[192,96,128]{2,0,1:T(8,128)(2,1)} collective-permute-done((bf16[192,96,128]{2,0,1:T(8,128)(2,1)}, bf16[192,96,128]{2,0,1:T(8,128)(2,1)}, u32[]{:S(2)}, u32[]{:S(2)}) %collective-permute-start.4) | collective-permute-done | bytes 4718624 | tf_op jit(solution)/shard_map/ppermute | solution.py:236
  550.6 7.6 copy.21
  558.2 92.4 %collective-permute-done.5 = bf16[192,96,128]{2,0,1:T(8,128)(2,1)} collective-permute-done((bf16[192,96,128]{2,0,1:T(8,128)(2,1)S(1)}, bf16[192,96,128]{2,0,1:T(8,128)(2,1)}, u32[]{:S(2)}, u32[]{:S(2)}) %collective-permute-start.5) | collective-permute-done | bytes 4718624 | tf_op jit(solution)/shard_map/ppermute | solution.py:236
  650.6 7.5 copy.22
  658.1 163.4 %all-to-all-done = bf16[192,96,1024]{2,1,0:T(8,128)(2,1)} async-done(((bf16[192,96,1024]{2,1,0:T(8,128)(2,1)}), bf16[192,96,1024]{2,1,0:T(8,128)(2,1)}, u32[]{:S(2)}, u32[]{:S(2)}) %all-to-all-start) | async-done | bytes 37748768 | tf_op jit(solution)/shard_map/all_to_all | solution.py:254
  821.5 5.5 shard_map.74
  827.1 3.8 collective-permute-start.10
  832.1 2.6 collective-permute-start.12
  834.7 32.1 %shard_map.73 = bf16[8,20,96,1024]{3,2,1,0:T(8,128)(2,1)} custom-call(bf16[768,768]{1,0:T(8,128)(2,1)} %bitcast.112, bf16[8,24,96,1024]{3,2,1,0:T(8,128)(2,1)} %bitcast.15.field_ref), custom_call_target="tpu_custom_call" | custom-call | flops 24159191040 | bytes 62914560 | tf_op jit(solution)/shard_map/pallas_call | solution.py:30
  866.8 5.8 collective-permute-done.9.refs_4_
  872.7 8.2 collective-permute-done.10.refs_5_
  881.9 19.2 %all-to-all-start.2 = ((bf16[160,96,1024]{2,1,0:T(8,128)(2,1)}), bf16[160,96,1024]{2,1,0:T(8,128)(2,1)}, u32[]{:S(2)}, u32[]{:S(2)}) async-start(bf16[160,96,1024]{2,1,0:T(8,128)(2,1)} %bitcast.94), calls=%async_computation.2 | async-start | bytes 62914560 | tf_op jit(solution)/shard_map/all_to_all | solution.py:302
  903.8 2.0 collective-permute-start.13
  905.8 4.2 collective-permute-start.14
  910.0 7.6 copy.27
  917.9 6.5 shard_map.75
  924.4 7.5 copy.28
  931.9 74.3 %collective-permute-done.17 = bf16[192,96,128]{2,0,1:T(8,128)(2,1)} collective-permute-done((bf16[192,96,128]{2,0,1:T(8,128)(2,1)}, bf16[192,96,128]{2,0,1:T(8,128)(2,1)}, u32[]{:S(2)}, u32[]{:S(2)}) %collective-permute-start.17) | collective-permute-done | bytes 4718624 | tf_op jit(solution)/shard_map/ppermute | solution.py:236
  1006.2 7.5 copy.29
  1013.7 92.8 %collective-permute-done.18 = bf16[192,96,128]{2,0,1:T(8,128)(2,1)} collective-permute-done((bf16[192,96,128]{2,0,1:T(8,128)(2,1)}, bf16[192,96,128]{2,0,1:T(8,128)(2,1)}, u32[]{:S(2)}, u32[]{:S(2)}) %collective-permute-start.18) | collective-permute-done | bytes 4718624 | tf_op jit(solution)/shard_map/ppermute | solution.py:236
  1106.4 7.9 copy.30
  1114.3 8.7 shard_map.77.base_ref
  1123.0 39.4 %collective-permute-done.13.refs_1_ = bf16[2,96,1024]{2,1,0:T(8,128)(2,1)S(1)} collective-permute-done((bf16[2,96,1024]{2,1,0:T(8,128)(2,1)}, bf16[2,96,1024]{2,1,0:T(8,128)(2,1)S(1)}, u32[]{:S(2)}, u32[]{:S(2)}) %collective-permute-start.13) | collective-permute-done | bytes 393248 | tf_op jit(solution)/shard_map/ppermute | solution.py:236
  1162.3 256.1 %collective-permute-done.14.refs_2_ = bf16[2,96,1024]{2,1,0:T(8,128)(2,1)S(1)} collective-permute-done((bf16[2,96,1024]{2,1,0:T(8,128)(2,1)S(1)}, bf16[2,96,1024]{2,1,0:T(8,128)(2,1)S(1)}, u32[]{:S(2)}, u32[]{:S(2)}) %collective-permute-start.14) | collective-permute-done | bytes 393248 | tf_op jit(solution)/shard_map/ppermute | solution.py:236
  1418.4 7.2 collective-permute-done.15.refs_3_
  1426.3 9.2 shard_map.76.refs_9_
  1435.5 146.4 %all-to-all-done.2 = bf16[160,96,1024]{2,1,0:T(8,128)(2,1)} async-done(((bf16[160,96,1024]{2,1,0:T(8,128)(2,1)}), bf16[160,96,1024]{2,1,0:T(8,128)(2,1)}, u32[]{:S(2)}, u32[]{:S(2)}) %all-to-all-start.2) | async-done | bytes 31457312 | tf_op jit(solution)/shard_map/all_to_all | solution.py:302
  1581.9 8.5 all-to-all-start.1
  1590.4 53.0 %shard_map.78.so_far_ref = bf16[8,24,96,1024]{3,2,1,0:T(8,128)(2,1)} custom-call(s32[2]{0:T(128)} %pad_add_fusion.place_ref, bf16[1024,1024]{1,0:T(8,128)(2,1)} %operator_ref.5, bf16[8,24,96,1024]{3,2,1,0:T(8,128)(2,1)} %bitcast.69, bf16[8,20,96,1024]{3,2,1,0:T(8,128)(2,1)} %bitcast.36.refs_0_, ...), custom_call_target="tpu_custom_call", output_to_operand_aliasing={{}: (12, {})} | custom-call | flops 32212254720 | bytes 125829120 | tf_op jit(solution)/shard_map/pallas_call | solution.py:138
  1643.4 18.0 %all-to-all-done.1 = bf16[16,96,1024]{2,1,0:T(8,128)(2,1)} async-done(((bf16[16,96,1024]{2,1,0:T(8,128)(2,1)}), bf16[16,96,1024]{2,1,0:T(8,128)(2,1)}, u32[]{:S(2)}, u32[]{:S(2)}) %all-to-all-start.1) | async-done | bytes 3145760 | tf_op jit(solution)/shard_map/all_to_all | solution.py:302
  1661.4 5.5 shard_map.79
  (79 shorter events, 11.1 us)
Async XLA Ops:
  0.0 821.5 %all-to-all-start = ((bf16[192,96,1024]{2,1,0:T(8,128)(2,1)}), bf16[192,96,1024]{2,1,0:T(8,128)(2,1)}, u32[]{:S(2)}, u32[]{:S(2)}) async-start(bf16[192,96,1024]{2,1,0:T(8,128)(2,1)} %param.7), calls=%async_computation | async-start | bytes 75497472 | tf_op jit(solution)/shard_map/all_to_all | solution.py:254
  33.8 15.9 slice-start.6
  33.8 20.1 %slice-start.4 = ((s8[4718592]{0:T(1024)(128)(4,1)}), s8[4194304]{0:T(1024)(128)(4,1)S(1)}, s32[]{:S(2)}) async-start(s8[4718592]{0:T(1024)(128)(4,1)} %bitcast.99), calls=%async_computation.7 | async-start | bytes 8388608
  40.2 104.9 %collective-permute-start.2 = (bf16[192,96,128]{2,0,1:T(8,128)(2,1)}, bf16[192,96,128]{2,0,1:T(8,128)(2,1)}, u32[]{:S(2)}, u32[]{:S(2)}) collective-permute-start(bf16[192,96,128]{2,0,1:T(8,128)(2,1)} %copy.39), channel_id=1, source_target_pairs={{0,24},{8,16},{16,8},{24,0},{1,25},{9,17},{17,9},{25,1},{2,26},{10... | collective-permute-start | bytes 14155784 | tf_op jit(solution)/shard_map/ppermute | solution.py:236
  42.6 7.1 slice-start.7
  42.6 11.3 slice-start.5
  49.2 198.1 %collective-permute-start.1 = (bf16[192,96,128]{2,0,1:T(8,128)(2,1)}, bf16[192,96,128]{2,0,1:T(8,128)(2,1)}, u32[]{:S(2)}, u32[]{:S(2)}) collective-permute-start(bf16[192,96,128]{2,0,1:T(8,128)(2,1)} %copy.38), channel_id=1, source_target_pairs={{0,16},{8,24},{16,0},{24,8},{1,17},{9,25},{17,1},{25,9},{2,18},{10... | collective-permute-start | bytes 14155784 | tf_op jit(solution)/shard_map/ppermute | solution.py:236
  49.7 9.5 slice-start.2
  53.8 193.5 %collective-permute-start = (bf16[192,96,128]{2,0,1:T(8,128)(2,1)}, bf16[192,96,128]{2,0,1:T(8,128)(2,1)}, u32[]{:S(2)}, u32[]{:S(2)}) collective-permute-start(bf16[192,96,128]{2,0,1:T(8,128)(2,1)} %copy.37), channel_id=1, source_target_pairs={{0,8},{8,0},{16,24},{24,16},{1,9},{9,1},{17,25},{25,17},{2,10},{10... | collective-permute-start | bytes 14155784 | tf_op jit(solution)/shard_map/ppermute | solution.py:236
  53.9 5.4 slice-start.3
  57.8 289.5 %collective-permute-start.8 = (bf16[192,96,128]{2,0,1:T(8,128)(2,1)}, bf16[192,96,128]{2,0,1:T(8,128)(2,1)}, u32[]{:S(2)}, u32[]{:S(2)}) collective-permute-start(bf16[192,96,128]{2,0,1:T(8,128)(2,1)} %copy.43), channel_id=1, source_target_pairs={{0,24},{8,16},{16,8},{24,0},{1,25},{9,17},{17,9},{25,1},{2,26},{10... | collective-permute-start | bytes 14155784 | tf_op jit(solution)/shard_map/ppermute | solution.py:236
  59.3 4.5 copy-start.2
  59.3 4.5 copy-start.11
  59.3 4.5 copy-start.12
  63.2 386.2 %collective-permute-start.7 = (bf16[192,96,128]{2,0,1:T(8,128)(2,1)}, bf16[192,96,128]{2,0,1:T(8,128)(2,1)}, u32[]{:S(2)}, u32[]{:S(2)}) collective-permute-start(bf16[192,96,128]{2,0,1:T(8,128)(2,1)} %copy.42), channel_id=1, source_target_pairs={{0,16},{8,24},{16,0},{24,8},{1,17},{9,25},{17,1},{25,9},{2,18},{10... | collective-permute-start | bytes 14155784 | tf_op jit(solution)/shard_map/ppermute | solution.py:236
  80.9 268.8 %copy-start = (bf16[768,768]{0,1:T(8,128)(2,1)}, bf16[768,768]{0,1:T(8,128)(2,1)S(1)}, u32[]{:S(2)}) copy-start(bf16[768,768]{0,1:T(8,128)(2,1)S(1)} %copy.10) | copy-start | bytes 3538948
  90.1 10.6 slice-start
  94.2 6.5 slice-start.1
  145.1 304.4 %collective-permute-start.6 = (bf16[192,96,128]{2,0,1:T(8,128)(2,1)}, bf16[192,96,128]{2,0,1:T(8,128)(2,1)}, u32[]{:S(2)}, u32[]{:S(2)}) collective-permute-start(bf16[192,96,128]{2,0,1:T(8,128)(2,1)} %copy.41), channel_id=1, source_target_pairs={{0,8},{8,0},{16,24},{24,16},{1,9},{9,1},{17,25},{25,17},{2,10},{10... | collective-permute-start | bytes 14155784 | tf_op jit(solution)/shard_map/ppermute | solution.py:236
  279.2 204.4 %collective-permute-start.3 = (bf16[192,96,128]{2,0,1:T(8,128)(2,1)}, bf16[192,96,128]{2,0,1:T(8,128)(2,1)}, u32[]{:S(2)}, u32[]{:S(2)}) collective-permute-start(bf16[192,96,128]{2,0,1:T(8,128)(2,1)} %get-tuple-element.71), channel_id=1, source_target_pairs={{0,8},{8,0},{16,24},{24,16},{1,9},{9,1},{17,25},{25,17},{2,10},{10... | collective-permute-start | bytes 14155784 | tf_op jit(solution)/shard_map/ppermute | solution.py:236
  279.2 271.3 %collective-permute-start.4 = (bf16[192,96,128]{2,0,1:T(8,128)(2,1)}, bf16[192,96,128]{2,0,1:T(8,128)(2,1)}, u32[]{:S(2)}, u32[]{:S(2)}) collective-permute-start(bf16[192,96,128]{2,0,1:T(8,128)(2,1)} %get-tuple-element.70), channel_id=1, source_target_pairs={{0,16},{8,24},{16,0},{24,8},{1,17},{9,25},{17,1},{25,9},{2,18},{10... | collective-permute-start | bytes 14155784 | tf_op jit(solution)/shard_map/ppermute | solution.py:236
  347.4 303.2 %collective-permute-start.5 = (bf16[192,96,128]{2,0,1:T(8,128)(2,1)S(1)}, bf16[192,96,128]{2,0,1:T(8,128)(2,1)}, u32[]{:S(2)}, u32[]{:S(2)}) collective-permute-start(bf16[192,96,128]{2,0,1:T(8,128)(2,1)S(1)} %get-tuple-element.69), channel_id=1, source_target_pairs={{0,24},{8,16},{16,8},{24,0},{1,25},{9,17},{17,9},{25,1},{2,26},{10... | collective-permute-start | bytes 14155784 | tf_op jit(solution)/shard_map/ppermute | solution.py:236
  349.7 5.2 copy-start.1
  349.7 99.8 %copy-start.3 = (bf16[768,4,192,1]{0,2,1,3:T(8,128)(2,1)S(1)}, bf16[768,4,192,1]{0,2,1,3:T(8,128)(2,1)}, u32[]{:S(2)}) copy-start(bf16[768,4,192,1]{0,2,1,3:T(8,128)(2,1)} %reshape.70) | copy-start | bytes 3538948
  827.1 45.6 %collective-permute-start.9 = (bf16[2,96,1024]{2,1,0:T(8,128)(2,1)}, bf16[2,96,1024]{2,1,0:T(8,128)(2,1)S(1)}, u32[]{:S(2)}, u32[]{:S(2)}) collective-permute-start(bf16[2,96,1024]{2,1,0:T(8,128)(2,1)} %get-tuple-element.32), channel_id=1, source_target_pairs={{0,4},{1,5},{2,6},{3,7},{4,0},{5,1},{6,2},{7,3},{8,12},{9,13},{10,... | collective-permute-start | bytes 1179656 | tf_op jit(solution)/shard_map/ppermute | solution.py:236
  827.1 53.8 %collective-permute-start.10 = (bf16[2,96,1024]{2,1,0:T(8,128)(2,1)}, bf16[2,96,1024]{2,1,0:T(8,128)(2,1)S(1)}, u32[]{:S(2)}, u32[]{:S(2)}) collective-permute-start(bf16[2,96,1024]{2,1,0:T(8,128)(2,1)} %get-tuple-element.33), channel_id=1, source_target_pairs={{0,5},{1,4},{2,7},{3,6},{4,1},{5,0},{6,3},{7,2},{8,13},{9,12},{10,... | collective-permute-start | bytes 1179656 | tf_op jit(solution)/shard_map/ppermute | solution.py:236
  830.8 50.1 %collective-permute-start.11 = (bf16[2,96,1024]{2,1,0:T(8,128)(2,1)}, bf16[2,96,1024]{2,1,0:T(8,128)(2,1)S(1)}, u32[]{:S(2)}, u32[]{:S(2)}) collective-permute-start(bf16[2,96,1024]{2,1,0:T(8,128)(2,1)} %get-tuple-element.34), channel_id=1, source_target_pairs={{0,6},{1,7},{2,4},{3,5},{4,2},{5,3},{6,0},{7,1},{8,14},{9,15},{10,... | collective-permute-start | bytes 1179656 | tf_op jit(solution)/shard_map/ppermute | solution.py:236
  832.1 48.8 %collective-permute-start.12 = (bf16[2,96,1024]{2,1,0:T(8,128)(2,1)}, bf16[2,96,1024]{2,1,0:T(8,128)(2,1)S(1)}, u32[]{:S(2)}, u32[]{:S(2)}) collective-permute-start(bf16[2,96,1024]{2,1,0:T(8,128)(2,1)} %get-tuple-element.35), channel_id=1, source_target_pairs={{0,7},{1,6},{2,5},{3,4},{4,3},{5,2},{6,1},{7,0},{8,15},{9,14},{10,... | collective-permute-start | bytes 1179656 | tf_op jit(solution)/shard_map/ppermute | solution.py:236
  872.7 8.3 copy-start.4
  880.9 0.8 copy-start.5
  880.9 0.9 copy-start.6
  880.9 1.0 copy-start.7
  880.9 24.9 %copy-start.14 = (bf16[2,96,1024]{2,1,0:T(8,128)(2,1)S(1)}, bf16[2,96,1024]{2,1,0:T(8,128)(2,1)}, u32[]{:S(2)}) copy-start(bf16[2,96,1024]{2,1,0:T(8,128)(2,1)} %get-tuple-element.39) | copy-start | bytes 1179652
  881.9 700.0 %all-to-all-start.2 = ((bf16[160,96,1024]{2,1,0:T(8,128)(2,1)}), bf16[160,96,1024]{2,1,0:T(8,128)(2,1)}, u32[]{:S(2)}, u32[]{:S(2)}) async-start(bf16[160,96,1024]{2,1,0:T(8,128)(2,1)} %bitcast.94), calls=%async_computation.2 | async-start | bytes 62914560 | tf_op jit(solution)/shard_map/all_to_all | solution.py:302
  901.1 16.4 collective-permute-start.16
  901.2 105.0 %collective-permute-start.17 = (bf16[192,96,128]{2,0,1:T(8,128)(2,1)}, bf16[192,96,128]{2,0,1:T(8,128)(2,1)}, u32[]{:S(2)}, u32[]{:S(2)}) collective-permute-start(bf16[192,96,128]{2,0,1:T(8,128)(2,1)} %get-tuple-element.51), channel_id=1, source_target_pairs={{0,16},{8,24},{16,0},{24,8},{1,17},{9,25},{17,1},{25,9},{2,18},{10... | collective-permute-start | bytes 14155784 | tf_op jit(solution)/shard_map/ppermute | solution.py:236
  902.4 204.0 %collective-permute-start.18 = (bf16[192,96,128]{2,0,1:T(8,128)(2,1)}, bf16[192,96,128]{2,0,1:T(8,128)(2,1)}, u32[]{:S(2)}, u32[]{:S(2)}) collective-permute-start(bf16[192,96,128]{2,0,1:T(8,128)(2,1)} %get-tuple-element.52), channel_id=1, source_target_pairs={{0,24},{8,16},{16,8},{24,0},{1,25},{9,17},{17,9},{25,1},{2,26},{10... | collective-permute-start | bytes 14155784 | tf_op jit(solution)/shard_map/ppermute | solution.py:236
  903.8 258.6 %collective-permute-start.13 = (bf16[2,96,1024]{2,1,0:T(8,128)(2,1)}, bf16[2,96,1024]{2,1,0:T(8,128)(2,1)S(1)}, u32[]{:S(2)}, u32[]{:S(2)}) collective-permute-start(bf16[2,96,1024]{2,1,0:T(8,128)(2,1)} %get-tuple-element.38), channel_id=1, source_target_pairs={{0,1},{1,0},{2,3},{3,2},{4,5},{5,4},{6,7},{7,6},{8,9},{9,8},{10,11... | collective-permute-start | bytes 1179656 | tf_op jit(solution)/shard_map/ppermute | solution.py:236
  905.8 11.8 copy-start.13
  905.8 512.6 %collective-permute-start.14 = (bf16[2,96,1024]{2,1,0:T(8,128)(2,1)S(1)}, bf16[2,96,1024]{2,1,0:T(8,128)(2,1)S(1)}, u32[]{:S(2)}, u32[]{:S(2)}) collective-permute-start(bf16[2,96,1024]{2,1,0:T(8,128)(2,1)S(1)} %copy-done.14), channel_id=1, source_target_pairs={{0,2},{1,3},{2,0},{3,1},{4,6},{5,7},{6,4},{7,5},{8,10},{9,11},{10,... | collective-permute-start | bytes 1179656 | tf_op jit(solution)/shard_map/ppermute | solution.py:236
  917.5 508.0 %collective-permute-start.15 = (bf16[2,96,1024]{2,1,0:T(8,128)(2,1)S(1)}, bf16[2,96,1024]{2,1,0:T(8,128)(2,1)S(1)}, u32[]{:S(2)}, u32[]{:S(2)}) collective-permute-start(bf16[2,96,1024]{2,1,0:T(8,128)(2,1)S(1)} %copy-done.13), channel_id=1, source_target_pairs={{0,3},{1,2},{2,1},{3,0},{4,7},{5,6},{6,5},{7,4},{8,11},{9,10},{10,... | collective-permute-start | bytes 1179656 | tf_op jit(solution)/shard_map/ppermute | solution.py:236
  1162.3 263.2 %copy-start.8 = (bf16[2,96,1024]{2,1,0:T(8,128)(2,1)}, bf16[2,96,1024]{2,1,0:T(8,128)(2,1)S(1)}, u32[]{:S(2)}) copy-start(bf16[2,96,1024]{2,1,0:T(8,128)(2,1)S(1)} %collective-permute-done.13.refs_1_) | copy-start | bytes 1179652
  1418.4 7.2 copy-start.9
  1425.6 0.8 copy-start.10
  1581.9 79.5 %all-to-all-start.1 = ((bf16[16,96,1024]{2,1,0:T(8,128)(2,1)}), bf16[16,96,1024]{2,1,0:T(8,128)(2,1)}, u32[]{:S(2)}, u32[]{:S(2)}) async-start(bf16[16,96,1024]{2,1,0:T(8,128)(2,1)} %bitcast.103), calls=%async_computation.1 | async-start | bytes 6291456 | tf_op jit(solution)/shard_map/all_to_all | solution.py:302
